TPU v7x, 1024 devices: a whole 4x8x16 slice. The times are simulated.
1024 devices in a mesh: island: 4 (over x_hi, core), fsdp: 16 (over z), tensor: 16 (over x_lo, y).
Axes of the slice: x: 4 (x_hi: 2, x_lo: 2; x = x_hi * 2 + x_lo), y: 8, z: 16, core: 2. Of those that a mesh axis runs over, the one named last changes fastest.
Arguments:
- tokens: bfloat16 [16384, 4608], P(('island', 'fsdp')), may hold values from -6 to 6
- cotangent: bfloat16 [16384, 4608], P(('island', 'fsdp')), may hold values from -0.19921875 to 0.19921875
- gate_tiles: bfloat16 [64, 16, 128, 128], P('fsdp', 'tensor'), may hold values from -0.25 to 0.25
- up_tiles: bfloat16 [64, 16, 128, 128], P('fsdp', 'tensor'), may hold values from -0.25 to 0.25
- gate_where: int32 [64, 16], P('fsdp', 'tensor'), may hold values from 0 to 647, as said below
- up_where: int32 [64, 16], P('fsdp', 'tensor'), may hold values from 0 to 647, as said below
- down_where: int32 [64, 16], P(None, 'tensor'), may hold values from 0 to 647, as said below
- down_global: float32 [64, 16, 128, 128], P('fsdp', 'tensor'), may hold values from -6 to 6
- down_moment: float32 [64, 16, 128, 128], P('fsdp', 'tensor'), may hold values from -3 to 3
Outputs:
- new_global: float32 [64, 16, 128, 128], P('fsdp', 'tensor')
- new_moment: float32 [64, 16, 128, 128], P('fsdp', 'tensor')
Inputs may be any that keep to these rules, and one draw needn't show every extreme that they name: In each column t, the 64 entries of gate_where are distinct cells r * 18 + c of the 36 x 18 tile grid of shard t (r a block of the model width, c a block of the shard's hidden units). In each column t, the 64 entries of up_where are distinct cells r * 18 + c of the 36 x 18 tile grid of shard t. In each column t, the 64 entries of down_where are distinct cells a * 36 + b, a a block of shard t's hidden units (18 of them) and b a block of the model width.
All inputs are finite; a program needn't handle non-finite values.
Results may differ from a plain program's by a relative error of at most 0.00057.
Values may be sent and summed in bfloat16 or wider, within the bound.
No kernel may reach another device: no remote copies, remote signals or barrier semaphores. Data moves between devices by JAX's collectives and lax.ppermute only.
A program may use at most 128 MiB of HBM per device.

v0:
```python
import jax
import jax.numpy as jnp
from jax import lax
from jax.sharding import PartitionSpec as P

FF = 36864


inner_rate = 0.5
decay_rate = 0.1
outer_rate = 0.7
momentum_rate = 0.9


def merge_tiles(total, tok_blocks, tiles, where, col_blocks):
    row_ids = where // col_blocks
    col_ids = where % col_blocks
    picked = jnp.take(tok_blocks, row_ids, axis=1)
    partial_value = jnp.einsum("tkr,krc->tkc", picked, tiles, preferred_element_type=jnp.float32)
    return total.at[:, col_ids].add(partial_value)


def body(
    tokens,
    cotangent,
    gate_tiles,
    up_tiles,
    gate_where,
    up_where,
    down_where,
    down_global,
    down_moment,
):
    count_rows = tokens.shape[0]
    tile_side = gate_tiles.shape[2]
    row_blocks = tokens.shape[1] // tile_side
    col_blocks = FF // tile_side // lax.axis_size("tensor")
    tok_blocks = tokens.reshape(count_rows, row_blocks, tile_side)
    cot_blocks = cotangent.reshape(count_rows, row_blocks, tile_side)
    zero_init = jnp.zeros((count_rows, col_blocks, tile_side), jnp.float32)
    gate_piece = lax.all_gather(gate_tiles, "fsdp", axis=0, tiled=True)
    up_piece = lax.all_gather(up_tiles, "fsdp", axis=0, tiled=True)
    gate_at = lax.all_gather(gate_where, "fsdp", axis=0, tiled=True)
    up_at = lax.all_gather(up_where, "fsdp", axis=0, tiled=True)
    gate_more = merge_tiles(zero_init, tok_blocks, gate_piece[:, 0], gate_at[:, 0], col_blocks)
    up_more = merge_tiles(zero_init, tok_blocks, up_piece[:, 0], up_at[:, 0], col_blocks)
    hidden = (jax.nn.silu(gate_more) * up_more).astype(jnp.bfloat16)
    places = down_where[:, 0]
    master = down_global[:, 0]
    moment = down_moment[:, 0]
    islands = lax.axis_size("island")
    hidden_pick = jnp.take(hidden, places // row_blocks, axis=1)
    cot_pick = jnp.take(cot_blocks, places % row_blocks, axis=1)
    summed = lax.psum_scatter(
        jnp.einsum("tka,tkb->kab", hidden_pick, cot_pick, preferred_element_type=jnp.float32),
        "fsdp",
        scatter_dimension=0,
        tiled=True,
    )
    delta_step = inner_rate * (summed + decay_rate * master)
    island_total = lax.psum(delta_step, "island")
    average = island_total / islands
    fresh_moment = momentum_rate * moment + average
    fresh_master = master - outer_rate * (average + momentum_rate * fresh_moment)
    return (fresh_master[:, None], fresh_moment[:, None])


def solution(mesh):
    placed = (
        P(("island", "fsdp"), None),
        P(("island", "fsdp"), None),
        P("fsdp", "tensor", None, None),
        P("fsdp", "tensor", None, None),
        P("fsdp", "tensor"),
        P("fsdp", "tensor"),
        P(None, "tensor"),
        P("fsdp", "tensor", None, None),
        P("fsdp", "tensor", None, None),
    )
    return jax.shard_map(
        body,
        mesh=mesh,
        in_specs=placed,
        out_specs=(P("fsdp", "tensor", None, None), P("fsdp", "tensor", None, None)),
        check_vma=False,
    )
```

profile of v0, /device:TPU:1, one launch (start us, length us, event | category | flops | bytes accessed | tf_op | source)
XLA Modules:
  0.0 356.8 jit_solution(15725625229834077232)
XLA Ops:
  7.2 0.7 all-gather.3.cloned.1.call-update
  7.9 0.7 all-gather.5.cloned.1.call-update
  8.7 4.3 %copy.26 = bf16[256,4608]{0,1:T(8,128)(2,1)} copy(bf16[256,4608]{1,0:T(8,128)(2,1)} %param.11) | data formatting | bytes 4718592 | tf_op args[0]
  13.0 3.0 copy.27
  16.0 1.3 dynamic-slice
  18.2 30.3 %all-reduce.2 = (s32[64]{0:T(128)S(1)}, s32[64]{0:T(128)S(1)}) all-reduce(s32[64]{0:T(128)S(1)} %bitcast_dynamic-update-slice_fusion, s32[64]{0:T(128)S(1)} %bitcast_dynamic-update-slice_fusion.1), channel_id=1, replica_groups=mesh['island'=4,'fsdp'=16,'tensor'=16] {'fsdp'}, use_global_device_ids=true, to_apply=%add.1 | all-reduce | flops 128 | bytes 1024
  48.5 3.0 gather_fusion.1
  51.5 3.0 gather_fusion.2
  54.6 4.3 %copy.29 = bf16[256,4608]{0,1:T(8,128)(2,1)} copy(bf16[256,4608]{1,0:T(8,128)(2,1)} %param.12) | data formatting | bytes 4718592 | tf_op args[1]
  58.8 3.0 copy.30
  61.9 3.1 gather_fusion.3
  65.0 22.2 %all-gather.3.cloned.1.call-done = bf16[64,1,128,128]{3,2,1,0:T(8,128)(2,1)} async-done(((bf16[4,1,128,128]{3,2,1,0:T(8,128)(2,1)}), bf16[64,1,128,128]{3,2,1,0:T(8,128)(2,1)}) %all-gather.3.cloned.1.call-update) | async-done | bytes 2097168 | tf_op jit(solution)/shard_map/all_gather | solution.py:41
  87.2 7.4 %fusion.5 = f32[64,256,128]{2,1,0:T(8,128)} fusion(bf16[64,256,128]{2,1,0:T(8,128)(2,1)} %gather_fusion.1, pred[64]{0:T(512)(128)(4,1)S(1)} %get-tuple-element.15, bf16[64,1,128,128]{3,2,1,0:T(8,128)(2,1)} %all-gather.3.cloned.1.call-done), kind=kOutput, calls=%fused_computation.11 | convolution fusion | flops 538968064 | bytes 14680128 | tf_op jit(solution)/shard_map/tkr,krc->tkc/dot_general | solution.py:19
  94.9 12.4 %scatter_fusion = f32[256,18,128]{2,0,1:T(8,128)S(1)} fusion(f32[256,18,128]{2,0,1:T(8,128)S(1)} %broadcast_in_dim.31.clone.1, s32[64]{0:T(128)S(1)} %get-tuple-element.21, f32[64,256,128]{2,1,0:T(8,128)} %fusion.5), kind=kCustom, calls=%fused_computation.4 | custom fusion | flops 2097152 | bytes 25166080 | tf_op jit(solution)/shard_map/scatter-add | solution.py:20
  107.3 55.9 %all-gather.5.cloned.1.call-done = bf16[64,1,128,128]{3,2,1,0:T(8,128)(2,1)} async-done(((bf16[4,1,128,128]{3,2,1,0:T(8,128)(2,1)}), bf16[64,1,128,128]{3,2,1,0:T(8,128)(2,1)}) %all-gather.5.cloned.1.call-update) | async-done | bytes 2097168 | tf_op jit(solution)/shard_map/all_gather | solution.py:42
  163.2 7.4 %fusion.3 = f32[64,256,128]{2,1,0:T(8,128)} fusion(bf16[64,256,128]{2,1,0:T(8,128)(2,1)} %gather_fusion.2, pred[64]{0:T(512)(128)(4,1)S(1)} %get-tuple-element.17, bf16[64,1,128,128]{3,2,1,0:T(8,128)(2,1)} %all-gather.5.cloned.1.call-done), kind=kOutput, calls=%fused_computation.9 | convolution fusion | flops 538968064 | bytes 14680128 | tf_op jit(solution)/shard_map/tkr,krc->tkc/dot_general | solution.py:19
  170.8 12.4 %scatter_fusion.1 = f32[256,18,128]{2,0,1:T(8,128)S(1)} fusion(f32[256,18,128]{2,0,1:T(8,128)S(1)} %broadcast_in_dim.31.clone, s32[64]{0:T(128)S(1)} %get-tuple-element.22, f32[64,256,128]{2,1,0:T(8,128)} %fusion.3), kind=kCustom, calls=%fused_computation.5 | custom fusion | flops 2097152 | bytes 25166080 | tf_op jit(solution)/shard_map/scatter-add | solution.py:20
  183.3 2.3 multiply_convert_fusion
  185.6 3.1 gather_fusion
  188.6 7.0 %fusion = f32[64,128,128]{2,1,0:T(8,128)} fusion(bf16[64,256,128]{2,1,0:T(8,128)(2,1)} %gather_fusion.3, bf16[64,256,128]{2,1,0:T(8,128)(2,1)} %gather_fusion, pred[64]{0:T(512)(128)(4,1)S(1)} %get-tuple-element.13, pred[64]{0:T(512)(128)(4,1)S(1)} %get-tuple-element.11), kind=kOutput, calls=%fused_computation.6 | convolution fusion | flops 541065216 | bytes 12583040 | tf_op jit(solution)/shard_map/tka,tkb->kab/dot_general | solution.py:55
  195.7 78.8 %reduce-scatter.2.cloned.1.call-done = f32[4,128,128]{2,1,0:T(8,128)} async-done(((f32[64,128,128]{2,1,0:T(8,128)}), f32[4,128,128]{2,1,0:T(8,128)}) %reduce-scatter.2.cloned.1.call-update) | async-done | bytes 262160 | tf_op jit(solution)/shard_map/reduce_scatter | solution.py:54
  274.6 1.7 fusion.21
  276.3 72.2 %all-reduce.5.cloned.1.call-done = f32[4,128,128]{2,1,0:T(8,128)} async-done(((f32[4,128,128]{2,1,0:T(8,128)}), f32[4,128,128]{2,1,0:T(8,128)}) %all-reduce.5.cloned.1.call-update) | async-done | bytes 262160 | tf_op jit(solution)/shard_map/psum | solution.py:61
  348.4 1.8 fusion.23
  (33 shorter events, 1.0 us)
Async XLA Ops:
  7.2 80.1 %all-gather.3.cloned.1.call-start = ((), (), s32[]{:S(2)}) async-start(), calls=%async_computation.1 | async-start | bytes 2228224 | tf_op jit(solution)/shard_map/all_gather | solution.py:41
  7.9 155.3 %all-gather.5.cloned.1.call-start = ((), (), s32[]{:S(2)}) async-start(), calls=%async_computation.2 | async-start | bytes 2228224 | tf_op jit(solution)/shard_map/all_gather | solution.py:42
  8.6 265.9 %reduce-scatter.2.cloned.1.call-start = ((), (), s32[]{:S(2)}) async-start(), calls=%async_computation.3 | async-start | bytes 4456448 | tf_op jit(solution)/shard_map/reduce_scatter | solution.py:54
  8.7 9.3 %copy-start.3 = (s32[4,1]{0,1:T(1,128)S(1)}, s32[4,1]{0,1:T(1,128)}, u32[]{:S(2)}) copy-start(s32[4,1]{0,1:T(1,128)} %param.16) | copy-start | bytes 52
  8.7 9.4 %copy-start.4 = (s32[4,1]{0,1:T(1,128)S(1)}, s32[4,1]{0,1:T(1,128)}, u32[]{:S(2)}) copy-start(s32[4,1]{0,1:T(1,128)} %param.15) | copy-start | bytes 52
  54.6 7.3 %copy-start.5 = (s32[64,1]{0,1:T(1,128)S(1)}, s32[64,1]{0,1:T(1,128)}, u32[]{:S(2)}) copy-start(s32[64,1]{0,1:T(1,128)} %param.17) | copy-start | bytes 772
  107.3 63.3 %copy-start = (f32[256,18,128]{2,0,1:T(8,128)}, f32[256,18,128]{2,0,1:T(8,128)S(1)}, u32[]{:S(2)}) copy-start(f32[256,18,128]{2,0,1:T(8,128)S(1)} %scatter_fusion) | copy-start | bytes 7077892
  195.7 78.9 %copy-start.1 = (f32[4,1,128,128]{3,2,1,0:T(8,128)S(1)}, f32[4,1,128,128]{3,2,1,0:T(8,128)}, u32[]{:S(2)}) copy-start(f32[4,1,128,128]{3,2,1,0:T(8,128)} %param.18) | copy-start | bytes 786436
  195.7 152.8 %copy-start.2 = (f32[4,1,128,128]{3,2,1,0:T(8,128)S(1)}, f32[4,1,128,128]{3,2,1,0:T(8,128)}, u32[]{:S(2)}) copy-start(f32[4,1,128,128]{3,2,1,0:T(8,128)} %param.19) | copy-start | bytes 786436
  195.7 152.8 %all-reduce.5.cloned.1.call-start = ((), (), s32[]{:S(2)}) async-start(), calls=%async_computation.4 | async-start | bytes 524288 | tf_op jit(solution)/shard_map/psum | solution.py:61
Sparse Core Ops, SparseCore 0:
  10.7 76.5 all-gather.2
  89.9 73.2 all-gather.4
  195.8 78.7 reduce-scatter.1
  278.5 69.8 all-reduce.4
where the time goes:
time: 358 us; the launch traced here: 357 us
  waiting for transfers between devices  231 us (65%)
  other arithmetic  30.8 us (9%)
  blocking collectives  30.3 us (8%)
  local copies, waits for them, and re-layouts  28.7 us (8%)
  matrix products  21.8 us (6%)
  between operations  14.6 us (4%)
    reduce_scatter x1, waiting for transfers between devices, body(): lax.psum_scatter(jnp.einsum('tka,tkb->kab', hidden_pick, cot_pick, prefer...  78.8 us
    psum x1, waiting for transfers between devices, body(): island_total = lax.psum(delta_step, 'island')  72.2 us
    all_gather x1, waiting for transfers between devices, body(): up_piece = lax.all_gather(up_tiles, 'fsdp', axis=0, tiled=True)  55.9 us
    unnamed x1, blocking collectives  30.3 us
    scatter-add x2, other arithmetic, merge_tiles(): return total.at[:, col_ids].add(partial_value)  24.9 us
    all_gather x1, waiting for transfers between devices, body(): gate_piece = lax.all_gather(gate_tiles, 'fsdp', axis=0, tiled=True)  22.2 us
    dot_general x2, matrix products, merge_tiles(): jnp.einsum('tkr,krc->tkc', picked, tiles, preferred_element_type=jnp.floa...  14.8 us
    unnamed x19, local copies, waits for them, and re-layouts  10 us
  transfers between devices with their start and end apart: 4, of which 4 were waited for; matrix products, arithmetic and copies ran while one was open for 13% of the time, Pallas kernels for 0%

commit v1 on v0

v1 whole, which is shorter than its diff:
```python
import jax
import jax.numpy as jnp
from jax import lax
from jax.experimental import pallas as pl
from jax.experimental.pallas import tpu as pltpu
from jax.sharding import PartitionSpec as P

FF = 36864
SIDE = 128
META = 16

inner_rate = 0.5
decay_rate = 0.1
outer_rate = 0.7
momentum_rate = 0.9

f32 = jnp.float32
bf16 = jnp.bfloat16


def block(index):
    return pl.ds(pl.multiple_of(index * SIDE, SIDE), SIDE)


def local_grads(col_blocks, row_blocks, each, cells, down, tok, cot, tiles, out, gate, up, hidden_t):
    gate[...] = jnp.zeros_like(gate)
    up[...] = jnp.zeros_like(up)
    owners = tiles.shape[0]

    def project(owner, carry):
        for k in range(2 * each):
            acc = gate if k < each else up
            row = cells[owner, k]
            col = cells[owner, 2 * each + k]
            acc[col] += jnp.dot(
                tok[:, block(row)], tiles[owner, k * SIDE:(k + 1) * SIDE, :], preferred_element_type=f32
            )
        return carry

    lax.fori_loop(0, owners, project, 0)

    def activate(col, carry):
        value = gate[col]
        hidden = value / (1.0 + jnp.exp(-value)) * up[col]
        hidden_t[block(col), :] = hidden.T.astype(bf16)
        return carry

    lax.fori_loop(0, col_blocks, activate, 0)

    def reduce_tokens(group, carry):
        for k in range(8):
            j = group * 8 + k
            place = down[j]
            out[j] = jnp.dot(
                hidden_t[block(place // row_blocks), :], cot[:, block(place % row_blocks)], preferred_element_type=f32
            )
        return carry

    lax.fori_loop(0, out.shape[0] // 8, reduce_tokens, 0)


def body(tokens, cotangent, gate_tiles, up_tiles, gate_where, up_where, down_where, down_global, down_moment):
    count, width = tokens.shape
    each = gate_tiles.shape[0]
    row_blocks = width // SIDE
    col_blocks = FF // SIDE // lax.axis_size("tensor")
    fsdp = lax.axis_size("fsdp")
    kept = each * fsdp

    where = jnp.concatenate([gate_where[:, 0], up_where[:, 0]])
    cells = jnp.concatenate([where // col_blocks, where % col_blocks])
    meta = jnp.broadcast_to(cells.astype(bf16)[:, None], (META, SIDE))
    payload = jnp.concatenate([gate_tiles.reshape(each * SIDE, SIDE), up_tiles.reshape(each * SIDE, SIDE), meta])
    tiles = lax.all_gather(payload, "fsdp", axis=0)
    all_cells = tiles[:, 2 * each * SIDE:, 0].astype(jnp.int32)

    vmem = pl.BlockSpec(memory_space=pltpu.VMEM)
    smem = pl.BlockSpec(memory_space=pltpu.SMEM)
    partial = pl.pallas_call(
        lambda *refs: local_grads(col_blocks, row_blocks, each, *refs),
        out_shape=jax.ShapeDtypeStruct((kept, SIDE, SIDE), f32),
        in_specs=[smem, smem, vmem, vmem, vmem],
        out_specs=vmem,
        scratch_shapes=[
            pltpu.VMEM((col_blocks, count, SIDE), f32),
            pltpu.VMEM((col_blocks, count, SIDE), f32),
            pltpu.VMEM((col_blocks * SIDE, count), bf16),
        ],
        compiler_params=pltpu.CompilerParams(vmem_limit_bytes=48 * 2**20),
        cost_estimate=pl.CostEstimate(
            flops=2 * 3 * kept * count * SIDE * SIDE, bytes_accessed=14 * 2**20, transcendentals=col_blocks * count * SIDE
        ),
        name="local_grads",
    )(all_cells, down_where[:, 0], tokens, cotangent, tiles)

    summed = lax.psum_scatter(partial, "fsdp", scatter_dimension=0, tiled=True)
    islands = lax.axis_size("island")
    total = summed
    for bit in (1, 2):
        total = total + lax.ppermute(total, "island", [(i, i ^ bit) for i in range(islands)])
    master = down_global[:, 0]
    moment = down_moment[:, 0]
    average = inner_rate * (total / islands + decay_rate * master)
    fresh_moment = momentum_rate * moment + average
    fresh_master = master - outer_rate * (average + momentum_rate * fresh_moment)
    return (fresh_master[:, None], fresh_moment[:, None])


def solution(mesh):
    placed = (
        P(("island", "fsdp"), None),
        P(("island", "fsdp"), None),
        P("fsdp", "tensor", None, None),
        P("fsdp", "tensor", None, None),
        P("fsdp", "tensor"),
        P("fsdp", "tensor"),
        P(None, "tensor"),
        P("fsdp", "tensor", None, None),
        P("fsdp", "tensor", None, None),
    )
    return jax.shard_map(
        body,
        mesh=mesh,
        in_specs=placed,
        out_specs=(P("fsdp", "tensor", None, None), P("fsdp", "tensor", None, None)),
        check_vma=False,
    )
```

time: 358 us -> 225 us (0.63)
  waiting for transfers between devices: 231 us -> 170 us
  blocking collectives: 30.3 us -> 0 us
  other arithmetic: 30.8 us -> 5.78 us
  local copies, waits for them, and re-layouts: 28.7 us -> 3.99 us
  matrix products: 21.8 us -> 0 us
  starting transfers between devices: 0.16 us -> 17 us
  Pallas kernels: 0 us -> 14 us
    psum x1 -> x0, waiting for transfers between devices: 72.2 us -> none  [body(): island_total = lax.psum(delta_step, 'island')]
    unnamed x1 -> x0, blocking collectives: 30.3 us -> none
    scatter-add x2 -> x0, other arithmetic: 24.9 us -> none  [merge_tiles(): return total.at[:, col_ids].add(partial_value)]
    dot_general x3 -> x0, matrix products: 21.8 us -> none  [the longest x2 14.8 us: merge_tiles(): jnp.einsum('tkr,krc->tkc', picked, tiles, preferred_element_type=jnp.floa...]
    ppermute x0 -> x2, starting transfers between devices: none -> 17 us  [body(): lax.ppermute(total, 'island', [(i, i ^ bit) for i in range(islands)])]
    pallas_call x0 -> x1, Pallas kernels: none -> 14 us  [body(): pl.pallas_call(lambda *refs: local_grads(col_blocks, row_blocks, each, *r...]
    gather x4 -> x0, local copies, waits for them, and re-layouts: 12.2 us -> none  [the longest x2 6.05 us: merge_tiles(): picked = jnp.take(tok_blocks, row_ids, axis=1)]
    ppermute x0 -> x2, waiting for transfers between devices: none -> 7.55 us  [body(): lax.ppermute(total, 'island', [(i, i ^ bit) for i in range(islands)])]
  transfers between devices with their start and end apart: 4 -> 4, of which waited for: 4 -> 4; matrix products, arithmetic and copies ran while one was open for 13% -> 0% of each run, Pallas kernels for 0% -> 0%
where the time goes in v1:
time: 225 us; the launch traced here: 224 us
  waiting for transfers between devices  170 us (76%)
  starting transfers between devices  17 us (8%)
  between operations  14.1 us (6%)
  Pallas kernels  14 us (6%)
  other arithmetic  5.78 us (3%)
  local copies, waits for them, and re-layouts  3.99 us (2%)
    all_gather x1, waiting for transfers between devices, body(): tiles = lax.all_gather(payload, 'fsdp', axis=0)  83.9 us
    reduce_scatter x1, waiting for transfers between devices, body(): summed = lax.psum_scatter(partial, 'fsdp', scatter_dimension=0, tiled=True)  78.2 us
    ppermute x2, starting transfers between devices, body(): lax.ppermute(total, 'island', [(i, i ^ bit) for i in range(islands)])  17 us
    pallas_call x1, Pallas kernels, body(): pl.pallas_call(lambda *refs: local_grads(col_blocks, row_blocks, each, *r...  14 us
    ppermute x2, waiting for transfers between devices, body(): lax.ppermute(total, 'island', [(i, i ^ bit) for i in range(islands)])  7.55 us
  transfers between devices with their start and end apart: 4, of which 4 were waited for; matrix products, arithmetic and copies ran while one was open for 0% of the time, Pallas kernels for 0%

profile of v1, /device:TPU:1, one launch (start us, length us, event | category | flops | bytes accessed | tf_op | source)
XLA Modules:
  0.0 224.5 jit_solution(746735196633739129)
XLA Ops:
  7.2 0.0 all-gather.3.cloned.1.call-start
  7.2 0.8 fusion.5
  8.0 0.1 pad_maximum_fusion
  8.0 1.9 maximum_maximum_fusion
  9.9 0.0 all-gather.3.cloned.1.call-update
  9.9 0.0 reduce-scatter.2.cloned.1.call-start
  10.0 83.9 %all-gather.3.cloned.1.call-done = bf16[16640,128]{1,0:T(8,128)(2,1)} async-done(((bf16[1040,128]{1,0:T(8,128)(2,1)}), bf16[16640,128]{1,0:T(8,128)(2,1)}) %all-gather.3.cloned.1.call-update) | async-done | bytes 4259856 | tf_op jit(solution)/shard_map/all_gather | solution.py:74
  93.8 1.2 convert_reduce_fusion.refs_0_
  95.0 0.0 copy-start
  95.0 1.7 copy-done
  96.7 0.0 copy-start.1
  96.7 1.7 copy-done.1
  98.4 0.7 copy-done.2
  99.0 14.0 %local_grads.1 = f32[64,128,128]{2,1,0:T(8,128)} custom-call(s32[16,16]{1,0:T(8,128)S(1)} %convert_reduce_fusion.refs_0_, s32[64]{0:T(128)S(1)} %bitcast.41, bf16[256,4608]{1,0:T(8,128)(2,1)S(1)} %copy-done, bf16[256,4608]{1,0:T(8,128)(2,1)S(1)} %copy-done.1, bf16[16,1040,128]{2,1,0:T(8,128)(2,1)} %bitcast.43), custom_call_target="tpu_custom_call" | custom-call | flops 1610612736 | bytes 14680064 | tf_op jit(solution)/shard_map/local_grads/pallas_call | solution.py:79
  113.0 0.0 reduce-scatter.2.cloned.1.call-update
  113.0 78.2 %reduce-scatter.2.cloned.1.call-done = f32[4,128,128]{2,1,0:T(8,128)} async-done(((f32[64,128,128]{2,1,0:T(8,128)}), f32[4,128,128]{2,1,0:T(8,128)}) %reduce-scatter.2.cloned.1.call-update) | async-done | bytes 262160 | tf_op jit(solution)/shard_map/reduce_scatter | solution.py:96
  191.2 11.9 %collective-permute-start = (f32[4,128,128]{2,1,0:T(8,128)}, f32[4,128,128]{2,1,0:T(8,128)S(1)}, u32[]{:S(2)}, u32[]{:S(2)}) collective-permute-start(f32[4,128,128]{2,1,0:T(8,128)} %reduce-scatter.2.cloned.1.call-done), channel_id=1, source_target_pairs={{0,256},{256,0},{512,768},{768,512},{1,257},{257,1},{513,769},{769... | collective-permute-start | bytes 786440 | tf_op jit(solution)/shard_map/ppermute | solution.py:100
  203.2 1.4 collective-permute-done
  204.5 1.0 add.29
  205.5 5.0 %collective-permute-start.1 = (f32[4,128,128]{2,1,0:T(8,128)S(1)}, f32[4,128,128]{2,1,0:T(8,128)S(1)}, u32[]{:S(2)}, u32[]{:S(2)}) collective-permute-start(f32[4,128,128]{2,1,0:T(8,128)S(1)} %add.29), channel_id=1, source_target_pairs={{0,512},{256,768},{512,0},{768,256},{1,513},{257,769},{513,1},{769... | collective-permute-start | bytes 786440 | tf_op jit(solution)/shard_map/ppermute | solution.py:100
  210.5 6.2 %collective-permute-done.1 = f32[4,128,128]{2,1,0:T(8,128)S(1)} collective-permute-done((f32[4,128,128]{2,1,0:T(8,128)S(1)}, f32[4,128,128]{2,1,0:T(8,128)S(1)}, u32[]{:S(2)}, u32[]{:S(2)}) %collective-permute-start.1) | collective-permute-done | bytes 262176 | tf_op jit(solution)/shard_map/ppermute | solution.py:100
  216.7 0.0 copy-done.3
  216.7 0.0 copy-done.4
  216.7 0.9 fusion.3
  (3 shorter events, 0.0 us)
Async XLA Ops:
  7.2 86.7 %all-gather.3.cloned.1.call-start = ((), (), s32[]{:S(2)}) async-start(), calls=%async_computation.2 | async-start | bytes 4526080 | tf_op jit(solution)/shard_map/all_gather | solution.py:74
  9.9 181.3 %reduce-scatter.2.cloned.1.call-start = ((), (), s32[]{:S(2)}) async-start(), calls=%async_computation.1 | async-start | bytes 4456448 | tf_op jit(solution)/shard_map/reduce_scatter | solution.py:96
  95.0 1.7 copy-start
  96.7 1.7 copy-start.1
  98.4 0.7 copy-start.2
  113.0 103.7 %copy-start.3 = (f32[4,1,128,128]{3,2,1,0:T(8,128)S(1)}, f32[4,1,128,128]{3,2,1,0:T(8,128)}, u32[]{:S(2)}) copy-start(f32[4,1,128,128]{3,2,1,0:T(8,128)} %param.17) | copy-start | bytes 786436
  113.0 103.7 %copy-start.4 = (f32[4,1,128,128]{3,2,1,0:T(8,128)S(1)}, f32[4,1,128,128]{3,2,1,0:T(8,128)}, u32[]{:S(2)}) copy-start(f32[4,1,128,128]{3,2,1,0:T(8,128)} %param.16) | copy-start | bytes 786436
  191.2 13.3 %collective-permute-start = (f32[4,128,128]{2,1,0:T(8,128)}, f32[4,128,128]{2,1,0:T(8,128)S(1)}, u32[]{:S(2)}, u32[]{:S(2)}) collective-permute-start(f32[4,128,128]{2,1,0:T(8,128)} %reduce-scatter.2.cloned.1.call-done), channel_id=1, source_target_pairs={{0,256},{256,0},{512,768},{768,512},{1,257},{257,1},{513,769},{769... | collective-permute-start | bytes 786440 | tf_op jit(solution)/shard_map/ppermute | solution.py:100
  205.5 11.2 %collective-permute-start.1 = (f32[4,128,128]{2,1,0:T(8,128)S(1)}, f32[4,128,128]{2,1,0:T(8,128)S(1)}, u32[]{:S(2)}, u32[]{:S(2)}) collective-permute-start(f32[4,128,128]{2,1,0:T(8,128)S(1)} %add.29), channel_id=1, source_target_pairs={{0,512},{256,768},{512,0},{768,256},{1,513},{257,769},{513,1},{769... | collective-permute-start | bytes 786440 | tf_op jit(solution)/shard_map/ppermute | solution.py:100
Sparse Core Ops, SparseCore 0:
  10.7 83.1 all-gather.2
  113.1 78.0 reduce-scatter.1

commit v2 on v1

v2 whole, which is shorter than its diff:
```python
import jax
import jax.numpy as jnp
from jax import lax
from jax.experimental import pallas as pl
from jax.experimental.pallas import tpu as pltpu
from jax.sharding import PartitionSpec as P

FF = 36864
SIDE = 128
META = 16
TILE_SCALE = 2.0**17
MARK = 8
TOP = 14

inner_rate = 0.5
decay_rate = 0.1
outer_rate = 0.7
momentum_rate = 0.9

f32 = jnp.float32
bf16 = jnp.bfloat16
f16 = jnp.float16


def block(index):
    return pl.ds(pl.multiple_of(index * SIDE, SIDE), SIDE)


def add_products(col_blocks, cells, tok, tiles, acc):
    owners, each = cells.shape

    def step(owner, carry):
        for k in range(each):
            cell = cells[owner, k]
            acc[cell % col_blocks] += jnp.dot(
                tok[:, block(cell // col_blocks)], tiles[owner, k * SIDE:(k + 1) * SIDE, :], preferred_element_type=f32
            )
        return carry

    lax.fori_loop(0, owners, step, 0)


def first_matrix(col_blocks, cells, tok, tiles, acc):
    acc[...] = jnp.zeros_like(acc)
    add_products(col_blocks, cells, tok, tiles, acc)


def token_sums(row_blocks, ranks, down, hidden_t, cot, out):
    halves, owners = out.shape[:2]

    def step(z, carry):
        for h in range(halves):
            place = down[z * 4 + ranks[h]]
            out[h, z] = jnp.dot(
                hidden_t[block(place // row_blocks), :], cot[:, block(place % row_blocks)], preferred_element_type=f32
            )
        return carry

    lax.fori_loop(0, owners, step, 0)


def second_matrix(col_blocks, row_blocks, cells, swapped, ranks, down, tok, tiles, first, cot, hidden_t, out, acc):
    acc[...] = jnp.zeros_like(acc)
    add_products(col_blocks, cells, tok, tiles, acc)
    first_is_gate = swapped[0] == 0

    def activate(col, carry):
        a, b = first[col], acc[col]
        gate = jnp.where(first_is_gate, a, b)
        up = jnp.where(first_is_gate, b, a)
        hidden = gate / (1.0 + jnp.exp(-gate)) * up
        hidden_t[block(col), :] = hidden.T.astype(bf16)
        return carry

    lax.fori_loop(0, col_blocks, activate, 0)
    token_sums(row_blocks, ranks, down, hidden_t, cot, out)


def call(kernel, out_shape, in_specs, scratch, flops, name):
    vmem = pl.BlockSpec(memory_space=pltpu.VMEM)
    return pl.pallas_call(
        kernel,
        out_shape=out_shape,
        in_specs=in_specs,
        out_specs=jax.tree.map(lambda _: vmem, out_shape),
        scratch_shapes=scratch,
        compiler_params=pltpu.CompilerParams(vmem_limit_bytes=20 * 2**20),
        cost_estimate=pl.CostEstimate(flops=flops, bytes_accessed=8 * 2**20, transcendentals=0),
        name=name,
    )


def narrow(values, rows):
    top = jnp.max(jnp.abs(values))
    power = jnp.clip(jnp.ceil(jnp.log2(top)), -100.0, 120.0)
    chunks = (values * jnp.exp2(TOP - power)).astype(f16).reshape(-1, rows, SIDE)
    mark = jnp.broadcast_to(power.astype(f16), (chunks.shape[0], MARK, SIDE))
    return jnp.concatenate([chunks, mark], axis=1)


def widen(chunks):
    rows = chunks.shape[1] - MARK
    power = chunks[:, rows, :1].astype(f32)
    return chunks[:, :rows].astype(f32) * jnp.exp2(power - TOP)[:, :, None]


def body(tokens, cotangent, gate_tiles, up_tiles, gate_where, up_where, down_where, down_global, down_moment):
    count, width = tokens.shape
    each = gate_tiles.shape[0]
    row_blocks = width // SIDE
    col_blocks = FF // SIDE // lax.axis_size("tensor")
    owners = lax.axis_size("fsdp")
    islands = lax.axis_size("island")
    me = lax.axis_index("island")
    core, column = me % 2, me // 2
    other_core = [(i, i ^ 1) for i in range(islands)]
    other_chip = [(i, i ^ 2) for i in range(islands)]

    is_gate = core == 0
    own = jnp.where(is_gate, gate_tiles, up_tiles).reshape(each * SIDE, SIDE)
    where = jnp.where(is_gate, gate_where, up_where)
    meta = jnp.broadcast_to(jnp.pad(where, ((0, META - each), (0, 0))).astype(f16), (META, SIDE))
    payload = jnp.concatenate([(own.astype(f32) * TILE_SCALE).astype(f16), meta])
    mine = lax.all_gather(payload, "fsdp", axis=0)
    theirs = lax.ppermute(mine, "island", other_core)

    def unpack(gathered):
        tiles = (gathered[:, :each * SIDE].astype(f32) * (1.0 / TILE_SCALE)).astype(bf16)
        return gathered[:, each * SIDE:each * SIDE + each, 0].astype(jnp.int32), tiles

    vmem = pl.BlockSpec(memory_space=pltpu.VMEM)
    smem = pl.BlockSpec(memory_space=pltpu.SMEM)
    blocks = jax.ShapeDtypeStruct((col_blocks, count, SIDE), f32)
    kept = each * owners
    down = down_where[:, 0]
    product = 2 * kept * count * SIDE * SIDE

    cells, tiles = unpack(mine)
    first = call(
        lambda *refs: first_matrix(col_blocks, *refs), blocks, [smem, vmem, vmem], [], product, "first_matrix"
    )(cells, tokens, tiles)
    cells, tiles = unpack(theirs)
    sums = jax.ShapeDtypeStruct((2, owners, SIDE, SIDE), f32)
    hidden_t, away = call(
        lambda *refs: second_matrix(col_blocks, row_blocks, *refs),
        (jax.ShapeDtypeStruct((col_blocks * SIDE, count), bf16), sums),
        [smem] * 4 + [vmem] * 4,
        [pltpu.VMEM(blocks.shape, f32)],
        product * 3 // 2,
        "second_matrix",
    )(cells, core[None], jnp.stack([column * 2 + 1 - core, (1 - column) * 2 + 1 - core]), down, tokens, tiles, first, cotangent)
    arrived = lax.ppermute(away, "island", other_core)
    stay = call(
        lambda *refs: token_sums(row_blocks, *refs), sums, [smem, smem, vmem, vmem], [], product // 2, "token_sums"
    )(jnp.stack([column * 2 + core, (1 - column) * 2 + core]), down, hidden_t, cotangent)

    chip = stay + arrived
    crossed = lax.ppermute(narrow(chip[1], owners * SIDE)[0], "island", other_chip)
    pair = chip[0] + widen(crossed[None]).reshape(owners, SIDE, SIDE)
    parts = lax.all_to_all(narrow(pair, SIDE), "fsdp", 0, 0, tiled=True)
    total = lax.all_gather(jnp.sum(widen(parts), axis=0), "island", axis=0)

    master = down_global[:, 0]
    moment = down_moment[:, 0]
    average = inner_rate * (total / islands + decay_rate * master)
    fresh_moment = momentum_rate * moment + average
    fresh_master = master - outer_rate * (average + momentum_rate * fresh_moment)
    return (fresh_master[:, None], fresh_moment[:, None])


def solution(mesh):
    placed = (
        P(("island", "fsdp"), None),
        P(("island", "fsdp"), None),
        P("fsdp", "tensor", None, None),
        P("fsdp", "tensor", None, None),
        P("fsdp", "tensor"),
        P("fsdp", "tensor"),
        P(None, "tensor"),
        P("fsdp", "tensor", None, None),
        P("fsdp", "tensor", None, None),
    )
    return jax.shard_map(
        body,
        mesh=mesh,
        in_specs=placed,
        out_specs=(P("fsdp", "tensor", None, None), P("fsdp", "tensor", None, None)),
        check_vma=False,
    )
```

time: 225 us -> 170 us (0.76)
  waiting for transfers between devices: 170 us -> 12.9 us
  blocking collectives: 0 us -> 100 us
  between operations: 14.1 us -> 3.06 us
  other arithmetic: 5.78 us -> 12.8 us
  Pallas kernels: 14 us -> 19.2 us
    all_gather x1 -> x0, waiting for transfers between devices: 83.9 us -> none  [body(): tiles = lax.all_gather(payload, 'fsdp', axis=0)]
    reduce_scatter x1 -> x0, waiting for transfers between devices: 78.2 us -> none  [body(): summed = lax.psum_scatter(partial, 'fsdp', scatter_dimension=0, tiled=True)]
    all_gather x0 -> x2, blocking collectives: none -> 65.1 us  [the longest x1 53.7 us: body(): mine = lax.all_gather(payload, 'fsdp', axis=0)]
    all_to_all x0 -> x1, blocking collectives: none -> 34.9 us  [body(): parts = lax.all_to_all(narrow(pair, SIDE), 'fsdp', 0, 0, tiled=True)]
    convert_element_type x1 -> x7, other arithmetic: 1.19 us -> 7.27 us  [the longest x2 4.32 us: unpack(): (gathered[:, :each * SIDE].astype(f32) * (1.0 / TILE_SCALE)).astype(bf16)]
    ppermute x2 -> x3, waiting for transfers between devices: 7.55 us -> 12.9 us  [the longest x1 12.2 us: body(): lax.ppermute(narrow(chip[1], owners * SIDE)[0], 'island', other_chip)]
    pallas_call x1 -> x3, Pallas kernels: 14 us -> 19.2 us  [the longest x1 11.1 us: body(): call(lambda *refs: second_matrix(col_blocks, row_blocks, *refs), (jax.Sha...]
    ppermute x2 -> x3, starting transfers between devices: 17 us -> 15.4 us  [the longest x1 8.87 us: body(): theirs = lax.ppermute(mine, 'island', other_core)]
  transfers between devices with their start and end apart: 4 -> 3, of which waited for: 4 -> 2; matrix products, arithmetic and copies ran while one was open for 0% -> 2% of each run, Pallas kernels for 0% -> 5%
where the time goes in v2:
time: 170 us; the launch traced here: 169 us
  blocking collectives  100 us (59%)
  Pallas kernels  19.2 us (11%)
  starting transfers between devices  15.4 us (9%)
  waiting for transfers between devices  12.9 us (8%)
  other arithmetic  12.8 us (8%)
  local copies, waits for them, and re-layouts  5.9 us (3%)
  between operations  3.06 us (2%)
    all_gather x1, blocking collectives, body(): mine = lax.all_gather(payload, 'fsdp', axis=0)  53.7 us
    all_to_all x1, blocking collectives, body(): parts = lax.all_to_all(narrow(pair, SIDE), 'fsdp', 0, 0, tiled=True)  34.9 us
    ppermute x1, waiting for transfers between devices, body(): lax.ppermute(narrow(chip[1], owners * SIDE)[0], 'island', other_chip)  12.2 us
    all_gather x1, blocking collectives, body(): total = lax.all_gather(jnp.sum(widen(parts), axis=0), 'island', axis=0)  11.4 us
    pallas_call x1, Pallas kernels, body(): call(lambda *refs: second_matrix(col_blocks, row_blocks, *refs), (jax.Sha...  11.1 us
    ppermute x1, starting transfers between devices, body(): theirs = lax.ppermute(mine, 'island', other_core)  8.87 us
    unnamed x16, local copies, waits for them, and re-layouts  4.76 us
    ppermute x1, starting transfers between devices, body(): lax.ppermute(narrow(chip[1], owners * SIDE)[0], 'island', other_chip)  4.65 us
  transfers between devices with their start and end apart: 3, of which 2 were waited for; matrix products, arithmetic and copies ran while one was open for 2% of the time, Pallas kernels for 5%

profile of v2, /device:TPU:1, one launch (start us, length us, event | category | flops | bytes accessed | tf_op | source)
XLA Modules:
  0.0 169.3 jit_solution(3337928039367329902)
XLA Ops:
  0.6 0.7 fusion.9
  1.3 1.0 multiply_convert_fusion.4
  2.5 53.7 %all-gather.3 = f16[8448,128]{1,0:T(8,128)(2,1)} all-gather(f16[528,128]{1,0:T(8,128)(2,1)S(1)} %pad_maximum_fusion), channel_id=2, replica_groups=mesh['island'=4,'fsdp'=16,'tensor'=16] {'fsdp'}, dimensions={0}, use_global_device_ids=true | all-gather | bytes 2297856 | tf_op jit(solution)/shard_map/all_gather | solution.py:124
  56.1 8.9 %collective-permute-start = (f16[16,528,128]{2,1,0:T(8,128)(2,1)}, f16[16,528,128]{2,1,0:T(8,128)(2,1)}, u32[]{:S(2)}, u32[]{:S(2)}) collective-permute-start(f16[16,528,128]{2,1,0:T(8,128)(2,1)} %bitcast.6), channel_id=1, source_target_pairs={{0,256},{256,0},{512,768},{768,512},{1,257},{257,1},{513,769},{769... | collective-permute-start | bytes 6488072 | tf_op jit(solution)/shard_map/ppermute | solution.py:125
  65.0 0.8 slice_convert_fusion
  66.0 2.2 %multiply_convert_fusion.refs_2_ = bf16[16,512,128]{2,1,0:T(8,128)(2,1)S(1)} fusion(f16[16,528,128]{2,1,0:T(8,128)(2,1)} %bitcast.6), kind=kLoop, calls=%fused_computation | loop fusion | flops 3145728 | bytes 4194304 | tf_op jit(solution)/shard_map/convert_element_type | solution.py:128
  68.2 4.5 %first_matrix.1.refs_6_ = f32[18,256,128]{2,1,0:T(8,128)S(1)} custom-call(s32[16,4]{1,0:T(8,128)S(1)} %copy.23.refs_0_, bf16[256,4608]{1,0:T(8,128)(2,1)S(1)} %copy-done.1, bf16[16,512,128]{2,1,0:T(8,128)(2,1)S(1)} %multiply_convert_fusion.refs_2_), custom_call_target="tpu_custom_call" | custom-call | flops 536870912 | bytes 8388608 | tf_op jit(solution)/shard_map/first_matrix/pallas_call | solution.py:139
  72.7 1.4 copy-done.3
  74.2 0.9 slice_convert_fusion.1
  75.3 2.2 %multiply_convert_fusion.1.refs_5_ = bf16[16,512,128]{2,1,0:T(8,128)(2,1)S(1)} fusion(f16[16,528,128]{2,1,0:T(8,128)(2,1)} %collective-permute-done), kind=kLoop, calls=%fused_computation.1 | loop fusion | flops 3145728 | bytes 4194304 | tf_op jit(solution)/shard_map/convert_element_type | solution.py:128
  77.5 1.7 copy-done.2
  79.1 1.7 copy-done.4
  80.8 11.1 %second_matrix.1 = (bf16[2304,256]{1,0:T(8,128)(2,1)S(1)}, f32[2,16,128,128]{3,2,1,0:T(8,128)}) custom-call(s32[16,4]{1,0:T(8,128)S(1)} %copy.24.refs_0_, s32[1]{0:T(128)} %bitcast.8.refs_1_, s32[2]{0:T(128)S(1)} %pad_add_fusion.1.refs_2_, s32[64]{0:T(128)S(1)} %bitcast.58, bf16[256,4608]{1,0:T(8,128)(2,1)S(1)} %copy-done.2, ...), custom_call_target="tpu_custom_call" | custom-call | flops 805306368 | bytes 8388608 | tf_op jit(solution)/shard_map/second_matrix/pallas_call | solution.py:144
  91.9 1.9 %collective-permute-start.1 = (f32[2,16,128,128]{3,2,1,0:T(8,128)}, f32[2,16,128,128]{3,2,1,0:T(8,128)}, u32[]{:S(2)}, u32[]{:S(2)}) collective-permute-start(f32[2,16,128,128]{3,2,1,0:T(8,128)} %get-tuple-element.5), channel_id=1, source_target_pairs={{0,256},{256,0},{512,768},{768,512},{1,257},{257,1},{513,769},{769... | collective-permute-start | bytes 6291464 | tf_op jit(solution)/shard_map/ppermute | solution.py:152
  93.9 3.6 %token_sums.1 = f32[2,16,128,128]{3,2,1,0:T(8,128)S(1)} custom-call(s32[2]{0:T(128)S(1)} %pad_add_fusion.refs_0_, s32[64]{0:T(128)S(1)} %bitcast.59, bf16[2304,256]{1,0:T(8,128)(2,1)S(1)} %get-tuple-element.4.refs_2_, bf16[256,4608]{1,0:T(8,128)(2,1)S(1)} %copy-done), custom_call_target="tpu_custom_call" | custom-call | flops 268435456 | bytes 8388608 | tf_op jit(solution)/shard_map/token_sums/pallas_call | solution.py:153
  97.5 0.7 collective-permute-done.1
  98.3 1.9 %add.49 = f32[2,16,128,128]{3,2,1,0:T(8,128)S(1)} add(f32[2,16,128,128]{3,2,1,0:T(8,128)S(1)} %token_sums.1, f32[2,16,128,128]{3,2,1,0:T(8,128)} %collective-permute-done.1) | non-fusion elementwise | flops 524288 | bytes 6291456 | tf_op jit(solution)/shard_map/add | solution.py:157
  100.2 0.7 abs_reduce_fusion.1
  101.9 4.6 %collective-permute-start.2 = (f16[2056,128]{1,0:T(8,128)(2,1)S(1)}, f16[2056,128]{1,0:T(8,128)(2,1)S(1)}, u32[]{:S(2)}, u32[]{:S(2)}) collective-permute-start(f16[2056,128]{1,0:T(8,128)(2,1)S(1)} %pad_bitcast_fusion), channel_id=1, source_target_pairs={{0,512},{256,768},{512,0},{768,256},{1,513},{257,769},{513,1},{769... | collective-permute-start | bytes 1579016 | tf_op jit(solution)/shard_map/ppermute | solution.py:158
  106.5 12.2 %collective-permute-done.2 = f16[2056,128]{1,0:T(8,128)(2,1)S(1)} collective-permute-done((f16[2056,128]{1,0:T(8,128)(2,1)S(1)}, f16[2056,128]{1,0:T(8,128)(2,1)S(1)}, u32[]{:S(2)}, u32[]{:S(2)}) %collective-permute-start.2) | collective-permute-done | bytes 526368 | tf_op jit(solution)/shard_map/ppermute | solution.py:158
  120.0 0.7 abs_reduce_fusion
  121.7 34.9 %all_to_all.5 = f16[16,136,128]{2,1,0:T(8,128)(2,1)S(1)} all-to-all(f16[16,136,128]{2,1,0:T(8,128)(2,1)S(1)} %concatenate.11), channel_id=1, replica_groups=mesh['island'=4,'fsdp'=16,'tensor'=16] {'fsdp'}, dimensions={0} | all-to-all | bytes 1114112 | tf_op jit(solution)/shard_map/all_to_all | solution.py:160
  157.0 11.4 %all-gather.1 = f32[512,128]{1,0:T(8,128)S(1)} all-gather(f32[128,128]{1,0:T(8,128)S(1)} %multiply_reduce_fusion), channel_id=3, replica_groups=mesh['island'=4,'fsdp'=16,'tensor'=16] {'island'}, dimensions={0}, use_global_device_ids=true | all-gather | bytes 327680 | tf_op jit(solution)/shard_map/all_gather | solution.py:161
  168.5 0.9 fusion.4
  (32 shorter events, 2.2 us)
Async XLA Ops:
  56.1 12.0 %copy-start.1 = (bf16[256,4608]{1,0:T(8,128)(2,1)S(1)}, bf16[256,4608]{1,0:T(8,128)(2,1)}, u32[]{:S(2)}) copy-start(bf16[256,4608]{1,0:T(8,128)(2,1)} %refs_4_.1) | copy-start | bytes 7077892
  56.1 18.0 %collective-permute-start = (f16[16,528,128]{2,1,0:T(8,128)(2,1)}, f16[16,528,128]{2,1,0:T(8,128)(2,1)}, u32[]{:S(2)}, u32[]{:S(2)}) collective-permute-start(f16[16,528,128]{2,1,0:T(8,128)(2,1)} %bitcast.6), channel_id=1, source_target_pairs={{0,256},{256,0},{512,768},{768,512},{1,257},{257,1},{513,769},{769... | collective-permute-start | bytes 6488072 | tf_op jit(solution)/shard_map/ppermute | solution.py:125
  72.7 1.4 copy-start.3
  74.1 3.4 %copy-start = (bf16[256,4608]{1,0:T(8,128)(2,1)S(1)}, bf16[256,4608]{1,0:T(8,128)(2,1)}, u32[]{:S(2)}) copy-start(bf16[256,4608]{1,0:T(8,128)(2,1)} %refs_3_.1) | copy-start | bytes 7077892
  74.1 3.4 %copy-start.5 = (s32[64,1]{0,1:T(1,128)S(1)}, s32[64,1]{0,1:T(1,128)}, u32[]{:S(2)}) copy-start(s32[64,1]{0,1:T(1,128)} %param.15) | copy-start | bytes 772
  77.5 1.7 copy-start.2
  79.1 1.7 copy-start.4
  91.9 6.4 %collective-permute-start.1 = (f32[2,16,128,128]{3,2,1,0:T(8,128)}, f32[2,16,128,128]{3,2,1,0:T(8,128)}, u32[]{:S(2)}, u32[]{:S(2)}) collective-permute-start(f32[2,16,128,128]{3,2,1,0:T(8,128)} %get-tuple-element.5), channel_id=1, source_target_pairs={{0,256},{256,0},{512,768},{768,512},{1,257},{257,1},{513,769},{769... | collective-permute-start | bytes 6291464 | tf_op jit(solution)/shard_map/ppermute | solution.py:152
  101.9 16.8 %collective-permute-start.2 = (f16[2056,128]{1,0:T(8,128)(2,1)S(1)}, f16[2056,128]{1,0:T(8,128)(2,1)S(1)}, u32[]{:S(2)}, u32[]{:S(2)}) collective-permute-start(f16[2056,128]{1,0:T(8,128)(2,1)S(1)} %pad_bitcast_fusion), channel_id=1, source_target_pairs={{0,512},{256,768},{512,0},{768,256},{1,513},{257,769},{513,1},{769... | collective-permute-start | bytes 1579016 | tf_op jit(solution)/shard_map/ppermute | solution.py:158
  121.6 46.9 %copy-start.6 = (f32[4,1,128,128]{3,2,1,0:T(8,128)S(1)}, f32[4,1,128,128]{3,2,1,0:T(8,128)}, u32[]{:S(2)}) copy-start(f32[4,1,128,128]{3,2,1,0:T(8,128)} %param.17) | copy-start | bytes 786436
  121.6 46.9 %copy-start.7 = (f32[4,1,128,128]{3,2,1,0:T(8,128)S(1)}, f32[4,1,128,128]{3,2,1,0:T(8,128)}, u32[]{:S(2)}) copy-start(f32[4,1,128,128]{3,2,1,0:T(8,128)} %param.16) | copy-start | bytes 786436

commit v3 on v2

v3 whole, which is shorter than its diff:
```python
import functools

import jax
import jax.numpy as jnp
from jax import lax
from jax.experimental import pallas as pl
from jax.experimental.pallas import tpu as pltpu
from jax.sharding import PartitionSpec as P

FF = 36864
SIDE = 128
META = 16
TILE_SCALE = 2.0**17
MARK = 8
TOP = 14

inner_rate = 0.5
decay_rate = 0.1
outer_rate = 0.7
momentum_rate = 0.9

f32 = jnp.float32
bf16 = jnp.bfloat16
f16 = jnp.float16


def block(index):
    return pl.ds(pl.multiple_of(index * SIDE, SIDE), SIDE)


def add_products(col_blocks, cells, base, tok, sent, tiles, sems, acc):
    owners = cells.shape[0]
    each = cells.shape[1] // 2
    together = 8
    groups = owners // together

    def fetch(group):
        part = pl.ds(group * together, together)
        return pltpu.make_async_copy(sent.at[part], tiles.at[part], sems.at[group])

    for group in range(groups):
        fetch(group).start()
    acc[...] = jnp.zeros_like(acc)
    for group in range(groups):
        fetch(group).wait()
        for owner in range(group * together, (group + 1) * together):
            for k in range(each):
                cell = cells[owner, base + k]
                acc[cell % col_blocks] += jnp.dot(
                    tok[:, block(cell // col_blocks)],
                    tiles[owner, k * SIDE:(k + 1) * SIDE, :],
                    preferred_element_type=f32,
                )


def first_matrix(col_blocks, cells, base, tok, sent, acc, tiles, sems):
    add_products(col_blocks, cells, base[0], tok, sent, tiles, sems, acc)


def token_sums(row_blocks, rank, down, hidden_t, cot, out):
    for z in range(out.shape[0]):
        place = down[z * 4 + rank[0]]
        out[z] = jnp.dot(
            hidden_t[block(place // row_blocks), :], cot[:, block(place % row_blocks)], preferred_element_type=f32
        )


def second_matrix(col_blocks, row_blocks, cells, base, rank, down, sent, tok, first, cot, hidden_t, out, acc, tiles, sems):
    add_products(col_blocks, cells, base[0], tok, sent, tiles, sems, acc)
    first_is_gate = base[0] != 0
    together = 6

    def activate(group, carry):
        for near in range(together):
            col = group * together + near
            a, b = first[col], acc[col]
            gate = jnp.where(first_is_gate, a, b)
            up = jnp.where(first_is_gate, b, a)
            hidden = gate / (1.0 + jnp.exp(-gate)) * up
            hidden_t[block(col), :] = hidden.astype(bf16).T
        return carry

    lax.fori_loop(0, col_blocks // together, activate, 0)
    token_sums(row_blocks, rank, down, hidden_t, cot, out)


def call(kernel, out_shape, in_specs, scratch, flops, name):
    vmem = pl.BlockSpec(memory_space=pltpu.VMEM)
    return pl.pallas_call(
        kernel,
        out_shape=out_shape,
        in_specs=in_specs,
        out_specs=jax.tree.map(lambda _: vmem, out_shape),
        scratch_shapes=scratch,
        compiler_params=pltpu.CompilerParams(vmem_limit_bytes=18 * 2**20),
        cost_estimate=pl.CostEstimate(flops=flops, bytes_accessed=8 * 2**20, transcendentals=0),
        name=name,
    )


def narrow(values):
    top = jnp.max(jnp.abs(values))
    power = jnp.clip(jnp.ceil(jnp.log2(top)), -100.0, 120.0)
    scaled = (values * jnp.exp2(TOP - power)).astype(f16).reshape(-1, SIDE)
    return jnp.concatenate([scaled, jnp.broadcast_to(power.astype(f16), (MARK, SIDE))])


def widen(sent):
    power = sent[-1, 0].astype(f32)
    return sent[:-MARK].astype(f32) * jnp.exp2(power - TOP)


def squeeze(values):
    root = 0.5 * jnp.sqrt(jnp.abs(values))
    return jnp.where(values < 0, -root, root).astype(f16)


def stretch(sent):
    root = sent.astype(f32)
    return 4.0 * root * jnp.abs(root)


def body(tokens, cotangent, gate_tiles, up_tiles, gate_where, up_where, down_where, down_global, down_moment):
    count, width = tokens.shape
    each = gate_tiles.shape[0]
    row_blocks = width // SIDE
    col_blocks = FF // SIDE // lax.axis_size("tensor")
    owners = lax.axis_size("fsdp")
    islands = lax.axis_size("island")
    me = lax.axis_index("island")
    core, column = me % 2, me // 2
    other_core = [(i, i ^ 1) for i in range(islands)]
    other_chip = [(i, i ^ 2) for i in range(islands)]

    own = jnp.where(core == 0, gate_tiles, up_tiles).reshape(each * SIDE, SIDE)
    where = jnp.concatenate([gate_where, up_where])
    meta = jnp.broadcast_to(jnp.pad(where, ((0, META - 2 * each), (0, 0))).astype(f16), (META, SIDE))
    gathered = lax.all_gather(
        jnp.concatenate([(own.astype(f32) * TILE_SCALE).astype(f16), meta]), "fsdp", axis=0
    )
    mine = (gathered[:, :each * SIDE].astype(f32) * (1.0 / TILE_SCALE)).astype(bf16)
    theirs = lax.ppermute(mine, "island", other_core)
    cells = gathered[:, each * SIDE:each * SIDE + 2 * each, 0].astype(jnp.int32)

    vmem = pl.BlockSpec(memory_space=pltpu.VMEM)
    smem = pl.BlockSpec(memory_space=pltpu.SMEM)
    far = pl.BlockSpec(memory_space=pl.ANY)
    blocks = jax.ShapeDtypeStruct((col_blocks, count, SIDE), f32)
    sums = jax.ShapeDtypeStruct((owners, SIDE, SIDE), f32)
    kept = each * owners
    down = down_where[:, 0]
    product = 2 * kept * count * SIDE * SIDE

    def sums_of(chip, side, hidden_t):
        kernel = functools.partial(token_sums, row_blocks)
        rank = (chip * 2 + side)[None]
        return call(kernel, sums, [smem, smem, vmem, vmem], [], product // 4, "token_sums")(rank, down, hidden_t, cotangent)

    staged = pltpu.VMEM(mine.shape, bf16)
    copies = pltpu.SemaphoreType.DMA((owners // 8,))
    first = call(
        functools.partial(first_matrix, col_blocks),
        blocks,
        [smem, smem, vmem, far],
        [staged, copies],
        product,
        "first_matrix",
    )(cells, (core * each)[None], tokens, mine)
    hidden_t, away = call(
        functools.partial(second_matrix, col_blocks, row_blocks),
        (jax.ShapeDtypeStruct((col_blocks * SIDE, count), bf16), sums),
        [smem] * 4 + [far] + [vmem] * 3,
        [pltpu.VMEM(blocks.shape, f32), staged, copies],
        product * 3 // 2,
        "second_matrix",
    )(cells, ((1 - core) * each)[None], ((1 - column) * 2 + 1 - core)[None], down, theirs, tokens, first, cotangent)

    arrived = lax.ppermute(away, "island", other_core)
    leaving = sums_of(1 - column, core, hidden_t) + arrived
    crossed = lax.ppermute(narrow(leaving), "island", other_chip)
    arrived = lax.ppermute(sums_of(column, 1 - core, hidden_t), "island", other_core)
    pair = sums_of(column, core, hidden_t) + arrived + widen(crossed).reshape(sums.shape)
    parts = lax.all_to_all(squeeze(pair), "fsdp", 0, 0, tiled=True)
    total = lax.all_gather(jnp.sum(stretch(parts), axis=0), "island", axis=0)

    master = down_global[:, 0]
    moment = down_moment[:, 0]
    average = inner_rate * (total / islands + decay_rate * master)
    fresh_moment = momentum_rate * moment + average
    fresh_master = master - outer_rate * (average + momentum_rate * fresh_moment)
    return (fresh_master[:, None], fresh_moment[:, None])


def solution(mesh):
    placed = (
        P(("island", "fsdp"), None),
        P(("island", "fsdp"), None),
        P("fsdp", "tensor", None, None),
        P("fsdp", "tensor", None, None),
        P("fsdp", "tensor"),
        P("fsdp", "tensor"),
        P(None, "tensor"),
        P("fsdp", "tensor", None, None),
        P("fsdp", "tensor", None, None),
    )
    return jax.shard_map(
        body,
        mesh=mesh,
        in_specs=placed,
        out_specs=(P("fsdp", "tensor", None, None), P("fsdp", "tensor", None, None)),
        check_vma=False,
    )
```

time: 170 us -> 157 us (0.924)
  blocking collectives: 100 us -> 92.1 us
  Pallas kernels: 19.2 us -> 13.6 us
  starting transfers between devices: 15.4 us -> 18 us
    all_to_all x1, blocking collectives: 34.9 us -> 26.2 us  [body(): parts = lax.all_to_all(squeeze(pair), 'fsdp', 0, 0, tiled=True)]
    pallas_call x3 -> x5, Pallas kernels: 19.2 us -> 13.6 us  [the longest x1 5.83 us: body(): call(functools.partial(second_matrix, col_blocks, row_blocks), (jax.Shape...]
    unnamed x16 -> x12, local copies, waits for them, and re-layouts: 4.76 us -> 1.7 us
    ppermute x1 -> x2, starting transfers between devices: 4.65 us -> 7.03 us  [the longest x1 4.64 us: body(): crossed = lax.ppermute(narrow(leaving), 'island', other_chip)]
    add x1 -> x0, other arithmetic: 1.89 us -> none  [body(): chip = stay + arrived]
    concatenate x1, local copies, waits for them, and re-layouts: 0.11 us -> 1.95 us  [narrow(): jnp.concatenate([scaled, jnp.broadcast_to(power.astype(f16), (MARK, SIDE))])]
    ppermute x1 -> x2, waiting for transfers between devices: 12.2 us -> 11.6 us  [the longest x1 11.6 us: body(): crossed = lax.ppermute(narrow(leaving), 'island', other_chip)]
    convert_element_type x6 -> x4, other arithmetic: 6.29 us -> 5.86 us  [the longest x1 2.15 us: narrow(): scaled = (values * jnp.exp2(TOP - power)).astype(f16).reshape(-1, SIDE)]
  transfers between devices with their start and end apart: 3 -> 4, of which waited for: 2 -> 1; matrix products, arithmetic and copies ran while one was open for 2% -> 6% of each run, Pallas kernels for 5% -> 5%
where the time goes in v3:
time: 157 us; the launch traced here: 156 us
  blocking collectives  92.1 us (59%)
  starting transfers between devices  18 us (11%)
  Pallas kernels  13.6 us (9%)
  other arithmetic  13.5 us (9%)
  waiting for transfers between devices  11.6 us (7%)
  local copies, waits for them, and re-layouts  4.96 us (3%)
  between operations  2.29 us (1%)
    all_gather x1, blocking collectives, body(): lax.all_gather(jnp.concatenate([(own.astype(f32) * TILE_SCALE).astype(f16...  51.7 us
    all_to_all x1, blocking collectives, body(): parts = lax.all_to_all(squeeze(pair), 'fsdp', 0, 0, tiled=True)  26.2 us
    all_gather x1, blocking collectives, body(): total = lax.all_gather(jnp.sum(stretch(parts), axis=0), 'island', axis=0)  14.3 us
    ppermute x1, waiting for transfers between devices, body(): crossed = lax.ppermute(narrow(leaving), 'island', other_chip)  11.6 us
    ppermute x1, starting transfers between devices, body(): theirs = lax.ppermute(mine, 'island', other_core)  9 us
    pallas_call x1, Pallas kernels, body(): call(functools.partial(second_matrix, col_blocks, row_blocks), (jax.Shape...  5.83 us
    ppermute x1, starting transfers between devices, body(): crossed = lax.ppermute(narrow(leaving), 'island', other_chip)  4.64 us
    pallas_call x3, Pallas kernels, sums_of(): call(kernel, sums, [smem, smem, vmem, vmem], [], product // 4, 'token_sums')  3.95 us
  transfers between devices with their start and end apart: 4, of which 1 were waited for; matrix products, arithmetic and copies ran while one was open for 6% of the time, Pallas kernels for 5%

profile of v3, /device:TPU:1, one launch (start us, length us, event | category | flops | bytes accessed | tf_op | source)
XLA Modules:
  0.0 156.0 jit_solution(6318731131569087292)
XLA Ops:
  0.6 0.7 convert.9
  2.1 1.0 multiply_convert_fusion.2
  3.2 51.7 %all-gather.3 = f16[8448,128]{1,0:T(8,128)(2,1)S(1)} all-gather(f16[528,128]{1,0:T(8,128)(2,1)S(1)} %pad_maximum_fusion), channel_id=2, replica_groups=mesh['island'=4,'fsdp'=16,'tensor'=16] {'fsdp'}, dimensions={0}, use_global_device_ids=true | all-gather | bytes 2297856 | tf_op jit(solution)/shard_map/all_gather | solution.py:138
  54.8 1.9 %multiply_convert_fusion.sent = bf16[16,512,128]{2,1,0:T(8,128)(2,1)} fusion(f16[16,528,128]{2,1,0:T(8,128)(2,1)S(1)} %bitcast.54), kind=kLoop, calls=%fused_computation | loop fusion | flops 3145728 | bytes 4194304 | tf_op jit(solution)/shard_map/convert_element_type | solution.py:141
  56.7 9.0 %collective-permute-start = (bf16[16,512,128]{2,1,0:T(8,128)(2,1)}, bf16[16,512,128]{2,1,0:T(8,128)(2,1)}, u32[]{:S(2)}, u32[]{:S(2)}) collective-permute-start(bf16[16,512,128]{2,1,0:T(8,128)(2,1)} %multiply_convert_fusion.sent), channel_id=1, source_target_pairs={{0,256},{256,0},{512,768},{768,512},{1,257},{257,1},{513,769},{769... | collective-permute-start | bytes 6291464 | tf_op jit(solution)/shard_map/ppermute | solution.py:142
  65.9 1.7 %copy-done.1 = bf16[256,4608]{1,0:T(8,128)(2,1)S(1)} copy-done((bf16[256,4608]{1,0:T(8,128)(2,1)S(1)}, bf16[256,4608]{1,0:T(8,128)(2,1)}, u32[]{:S(2)}) %copy-start.1) | copy-done | bytes 2359320
  67.6 3.8 %first_matrix.1.first = f32[18,256,128]{2,1,0:T(8,128)S(1)} custom-call(s32[16,8]{1,0:T(8,128)S(1)} %bitcast.48, s32[1]{0:T(128)} %bitcast.10.base, bf16[256,4608]{1,0:T(8,128)(2,1)S(1)} %copy-done.1, bf16[16,512,128]{2,1,0:T(8,128)(2,1)} %multiply_convert_fusion.sent), custom_call_target="tpu_custom_call" | custom-call | flops 536870912 | bytes 8388608 | tf_op jit(solution)/shard_map/first_matrix/pallas_call | solution.py:161
  71.4 5.8 %second_matrix.1 = (bf16[2304,256]{1,0:T(8,128)(2,1)S(1)}, f32[16,128,128]{2,1,0:T(8,128)}) custom-call(s32[16,8]{1,0:T(8,128)S(1)} %bitcast.49, s32[1]{0:T(128)} %bitcast.8.base, s32[1]{0:T(128)} %bitcast.9.rank, s32[64]{0:T(128)S(1)} %bitcast.50, bf16[16,512,128]{2,1,0:T(8,128)(2,1)} %collective-permute-done.sent, bf16[256,4608]{1,0:T(8,128)(2,1)S(1)} %copy-done.2, ...), custom_call_target="tpu_custom_call" | custom-call | flops 805306368 | bytes 8388608 | tf_op jit(solution)/shard_map/second_matrix/pallas_call | solution.py:169
  77.3 1.9 %collective-permute-start.2 = (f32[16,128,128]{2,1,0:T(8,128)}, f32[16,128,128]{2,1,0:T(8,128)}, u32[]{:S(2)}, u32[]{:S(2)}) collective-permute-start(f32[16,128,128]{2,1,0:T(8,128)} %get-tuple-element.5), channel_id=1, source_target_pairs={{0,256},{256,0},{512,768},{768,512},{1,257},{257,1},{513,769},{769... | collective-permute-start | bytes 3145736 | tf_op jit(solution)/shard_map/ppermute | solution.py:178
  79.2 2.0 %token_sums.4 = f32[16,128,128]{2,1,0:T(8,128)} custom-call(s32[1]{0:T(128)} %bitcast.11.rank, s32[64]{0:T(128)S(1)} %bitcast.51, bf16[2304,256]{1,0:T(8,128)(2,1)S(1)} %get-tuple-element.4.hidden_t, bf16[256,4608]{1,0:T(8,128)(2,1)S(1)} %copy-done), custom_call_target="tpu_custom_call" | custom-call | flops 134217728 | bytes 8388608 | tf_op jit(solution)/shard_map/token_sums/pallas_call | solution.py:157
  81.2 2.4 %collective-permute-start.1 = (f32[16,128,128]{2,1,0:T(8,128)}, f32[16,128,128]{2,1,0:T(8,128)}, u32[]{:S(2)}, u32[]{:S(2)}) collective-permute-start(f32[16,128,128]{2,1,0:T(8,128)} %token_sums.4), channel_id=1, source_target_pairs={{0,256},{256,0},{512,768},{768,512},{1,257},{257,1},{513,769},{769... | collective-permute-start | bytes 3145736 | tf_op jit(solution)/shard_map/ppermute | solution.py:181
  83.6 1.0 token_sums.5
  84.6 3.0 %abs_reduce_fusion = (f32[]{:T(128)}, f32[16,128,128]{2,1,0:T(8,128)}) fusion(f32[16,128,128]{2,1,0:T(8,128)S(1)} %token_sums.5, f32[16,128,128]{2,1,0:T(8,128)} %collective-permute-done.2), kind=kLoop, calls=%fused_computation.9 | loop fusion | flops 786431 | bytes 3145732 | tf_op jit(solution)/shard_map/reduce_max | solution.py:102
  88.3 2.1 %multiply_convert_fusion.1 = f16[16,128,128]{2,1,0:T(8,128)(2,1)} fusion(f32[16,128,128]{2,1,0:T(8,128)} %get-tuple-element.7, f32[]{:T(128)S(6)} %exp2.17), kind=kLoop, calls=%fused_computation.8 | loop fusion | flops 524288 | bytes 1572868 | tf_op jit(solution)/shard_map/convert_element_type | solution.py:104
  90.4 1.9 %concatenate.12 = f16[2056,128]{1,0:T(8,128)(2,1)} pad(f16[2048,128]{1,0:T(8,128)(2,1)} %bitcast.57, f16[]{:T(256)S(6)} %convert_element_type.49), padding=0_8x0_0 | pad | bytes 1050626 | tf_op jit(solution)/shard_map/concatenate | solution.py:105
  92.4 4.6 %collective-permute-start.3 = (f16[2056,128]{1,0:T(8,128)(2,1)}, f16[2056,128]{1,0:T(8,128)(2,1)}, u32[]{:S(2)}, u32[]{:S(2)}) collective-permute-start(f16[2056,128]{1,0:T(8,128)(2,1)} %concatenate.12), channel_id=1, source_target_pairs={{0,512},{256,768},{512,0},{768,256},{1,513},{257,769},{513,1},{769... | collective-permute-start | bytes 1579016 | tf_op jit(solution)/shard_map/ppermute | solution.py:180
  97.0 1.0 token_sums.3
  98.0 11.6 %collective-permute-done.3 = f16[2056,128]{1,0:T(8,128)(2,1)} collective-permute-done((f16[2056,128]{1,0:T(8,128)(2,1)}, f16[2056,128]{1,0:T(8,128)(2,1)}, u32[]{:S(2)}, u32[]{:S(2)}) %collective-permute-start.3) | collective-permute-done | bytes 526368 | tf_op jit(solution)/shard_map/ppermute | solution.py:180
  109.7 1.1 slice.19
  111.5 1.1 convert_multiply_fusion.1
  112.6 1.8 %fusion.2 = f16[16,128,128]{2,1,0:T(8,128)(2,1)S(1)} fusion(f32[16,128,128]{2,1,0:T(8,128)S(1)} %bitcast.56, f32[16,128,128]{2,1,0:T(8,128)S(1)} %token_sums.3, f32[16,128,128]{2,1,0:T(8,128)} %collective-permute-done.1), kind=kLoop, calls=%fused_computation.6 | loop fusion | flops 2097152 | bytes 3670016 | tf_op jit(solution)/shard_map/convert_element_type | solution.py:115
  114.5 26.2 %all_to_all.5 = f16[16,128,128]{2,1,0:T(8,128)(2,1)S(1)} all-to-all(f16[16,128,128]{2,1,0:T(8,128)(2,1)S(1)} %fusion.2), channel_id=1, replica_groups=mesh['island'=4,'fsdp'=16,'tensor'=16] {'fsdp'}, dimensions={0} | all-to-all | bytes 1048576 | tf_op jit(solution)/shard_map/all_to_all | solution.py:183
  140.8 14.3 %all-gather.1 = f32[512,128]{1,0:T(8,128)S(1)} all-gather(f32[128,128]{1,0:T(8,128)S(1)} %fusion.1), channel_id=3, replica_groups=mesh['island'=4,'fsdp'=16,'tensor'=16] {'island'}, dimensions={0}, use_global_device_ids=true | all-gather | bytes 327680 | tf_op jit(solution)/shard_map/all_gather | solution.py:184
  155.1 0.9 fusion.6
  (22 shorter events, 1.3 us)
Async XLA Ops:
  56.7 14.7 %collective-permute-start = (bf16[16,512,128]{2,1,0:T(8,128)(2,1)}, bf16[16,512,128]{2,1,0:T(8,128)(2,1)}, u32[]{:S(2)}, u32[]{:S(2)}) collective-permute-start(bf16[16,512,128]{2,1,0:T(8,128)(2,1)} %multiply_convert_fusion.sent), channel_id=1, source_target_pairs={{0,256},{256,0},{512,768},{768,512},{1,257},{257,1},{513,769},{769... | collective-permute-start | bytes 6291464 | tf_op jit(solution)/shard_map/ppermute | solution.py:142
  65.9 1.7 %copy-start.1 = (bf16[256,4608]{1,0:T(8,128)(2,1)S(1)}, bf16[256,4608]{1,0:T(8,128)(2,1)}, u32[]{:S(2)}) copy-start(bf16[256,4608]{1,0:T(8,128)(2,1)} %tok.3) | copy-start | bytes 7077892
  67.6 3.8 %copy-start = (bf16[256,4608]{1,0:T(8,128)(2,1)S(1)}, bf16[256,4608]{1,0:T(8,128)(2,1)}, u32[]{:S(2)}) copy-start(bf16[256,4608]{1,0:T(8,128)(2,1)} %cot.7) | copy-start | bytes 7077892
  67.6 3.8 %copy-start.2 = (bf16[256,4608]{1,0:T(8,128)(2,1)S(1)}, bf16[256,4608]{1,0:T(8,128)(2,1)}, u32[]{:S(2)}) copy-start(bf16[256,4608]{1,0:T(8,128)(2,1)} %tok.3) | copy-start | bytes 7077892
  67.6 3.8 %copy-start.3 = (s32[64,1]{0,1:T(1,128)S(1)}, s32[64,1]{0,1:T(1,128)}, u32[]{:S(2)}) copy-start(s32[64,1]{0,1:T(1,128)} %param.15) | copy-start | bytes 772
  77.3 7.3 %collective-permute-start.2 = (f32[16,128,128]{2,1,0:T(8,128)}, f32[16,128,128]{2,1,0:T(8,128)}, u32[]{:S(2)}, u32[]{:S(2)}) collective-permute-start(f32[16,128,128]{2,1,0:T(8,128)} %get-tuple-element.5), channel_id=1, source_target_pairs={{0,256},{256,0},{512,768},{768,512},{1,257},{257,1},{513,769},{769... | collective-permute-start | bytes 3145736 | tf_op jit(solution)/shard_map/ppermute | solution.py:178
  81.2 31.5 %collective-permute-start.1 = (f32[16,128,128]{2,1,0:T(8,128)}, f32[16,128,128]{2,1,0:T(8,128)}, u32[]{:S(2)}, u32[]{:S(2)}) collective-permute-start(f32[16,128,128]{2,1,0:T(8,128)} %token_sums.4), channel_id=1, source_target_pairs={{0,256},{256,0},{512,768},{768,512},{1,257},{257,1},{513,769},{769... | collective-permute-start | bytes 3145736 | tf_op jit(solution)/shard_map/ppermute | solution.py:181
  92.4 17.3 %collective-permute-start.3 = (f16[2056,128]{1,0:T(8,128)(2,1)}, f16[2056,128]{1,0:T(8,128)(2,1)}, u32[]{:S(2)}, u32[]{:S(2)}) collective-permute-start(f16[2056,128]{1,0:T(8,128)(2,1)} %concatenate.12), channel_id=1, source_target_pairs={{0,512},{256,768},{512,0},{768,256},{1,513},{257,769},{513,1},{769... | collective-permute-start | bytes 1579016 | tf_op jit(solution)/shard_map/ppermute | solution.py:180
  114.4 40.7 %copy-start.4 = (f32[4,1,128,128]{3,2,1,0:T(8,128)S(1)}, f32[4,1,128,128]{3,2,1,0:T(8,128)}, u32[]{:S(2)}) copy-start(f32[4,1,128,128]{3,2,1,0:T(8,128)} %param.17) | copy-start | bytes 786436
  114.4 40.7 %copy-start.5 = (f32[4,1,128,128]{3,2,1,0:T(8,128)S(1)}, f32[4,1,128,128]{3,2,1,0:T(8,128)}, u32[]{:S(2)}) copy-start(f32[4,1,128,128]{3,2,1,0:T(8,128)} %param.16) | copy-start | bytes 786436

commit v4 on v3

--- a/solution.py
+++ b/solution.py
@@ -11,8 +11,7 @@
 SIDE = 128
 META = 16
 TILE_SCALE = 2.0**17
-MARK = 8
-TOP = 14
+WHOLE = 15.0
 
 inner_rate = 0.5
 decay_rate = 0.1
@@ -57,7 +56,8 @@
     add_products(col_blocks, cells, base[0], tok, sent, tiles, sems, acc)
 
 
-def token_sums(row_blocks, rank, down, hidden_t, cot, out):
+def token_sums(row_blocks, rank, down, hidden_t, cot, *refs):
+    out = refs[-1]
     for z in range(out.shape[0]):
         place = down[z * 4 + rank[0]]
         out[z] = jnp.dot(
@@ -93,21 +93,26 @@
         out_specs=jax.tree.map(lambda _: vmem, out_shape),
         scratch_shapes=scratch,
         compiler_params=pltpu.CompilerParams(vmem_limit_bytes=18 * 2**20),
-        cost_estimate=pl.CostEstimate(flops=flops, bytes_accessed=8 * 2**20, transcendentals=0),
+        cost_estimate=pl.CostEstimate(flops=flops, bytes_accessed=8, transcendentals=0),
         name=name,
     )
 
 
-def narrow(values):
-    top = jnp.max(jnp.abs(values))
-    power = jnp.clip(jnp.ceil(jnp.log2(top)), -100.0, 120.0)
-    scaled = (values * jnp.exp2(TOP - power)).astype(f16).reshape(-1, SIDE)
-    return jnp.concatenate([scaled, jnp.broadcast_to(power.astype(f16), (MARK, SIDE))])
-
-
-def widen(sent):
-    power = sent[-1, 0].astype(f32)
-    return sent[:-MARK].astype(f32) * jnp.exp2(power - TOP)
+def to_whole(ours, theirs, out, powers):
+    owners = ours.shape[0]
+    for z in range(owners):
+        value = ours[z] + theirs[z]
+        top = jnp.max(jnp.abs(value), axis=0, keepdims=True)
+        power = jnp.floor(jnp.log2(jnp.maximum(top, 1e-30))) + 1.0
+        whole = jnp.round(value * jnp.exp2(WHOLE - power))
+        out[z * SIDE:(z + 1) * SIDE, :] = jnp.clip(whole, -32767.0, 32767.0).astype(jnp.int32).astype(jnp.int16)
+        powers[z:z + 1, :] = power
+    out[owners * SIDE:, :] = powers[...].astype(jnp.int32).astype(jnp.int16)
+
+
+def from_whole(sent, owners):
+    scale = jnp.exp2(sent[owners * SIDE:].astype(f32) - WHOLE)
+    return sent[:owners * SIDE].reshape(owners, SIDE, SIDE).astype(f32) * scale[:, None, :]
 
 
 def squeeze(values):
@@ -134,10 +139,9 @@
 
     own = jnp.where(core == 0, gate_tiles, up_tiles).reshape(each * SIDE, SIDE)
     where = jnp.concatenate([gate_where, up_where])
-    meta = jnp.broadcast_to(jnp.pad(where, ((0, META - 2 * each), (0, 0))).astype(f16), (META, SIDE))
-    gathered = lax.all_gather(
-        jnp.concatenate([(own.astype(f32) * TILE_SCALE).astype(f16), meta]), "fsdp", axis=0
-    )
+    meta = jnp.broadcast_to(jnp.pad(where, ((0, META - 2 * each), (0, 0))).astype(f32), (META, SIDE))
+    payload = jnp.concatenate([own.astype(f32) * TILE_SCALE, meta]).astype(f16)
+    gathered = lax.all_gather(payload, "fsdp", axis=0)
     mine = (gathered[:, :each * SIDE].astype(f32) * (1.0 / TILE_SCALE)).astype(bf16)
     theirs = lax.ppermute(mine, "island", other_core)
     cells = gathered[:, each * SIDE:each * SIDE + 2 * each, 0].astype(jnp.int32)
@@ -151,10 +155,12 @@
     down = down_where[:, 0]
     product = 2 * kept * count * SIDE * SIDE
 
-    def sums_of(chip, side, hidden_t):
+    def sums_of(chip, side, *after):
         kernel = functools.partial(token_sums, row_blocks)
         rank = (chip * 2 + side)[None]
-        return call(kernel, sums, [smem, smem, vmem, vmem], [], product // 4, "token_sums")(rank, down, hidden_t, cotangent)
+        return call(kernel, sums, [smem, smem, vmem, vmem] + [far] * len(after), [], 10**11, "token_sums")(
+            rank, down, hidden_t, cotangent, *after
+        )
 
     staged = pltpu.VMEM(mine.shape, bf16)
     copies = pltpu.SemaphoreType.DMA((owners // 8,))
@@ -176,10 +182,17 @@
     )(cells, ((1 - core) * each)[None], ((1 - column) * 2 + 1 - core)[None], down, theirs, tokens, first, cotangent)
 
     arrived = lax.ppermute(away, "island", other_core)
-    leaving = sums_of(1 - column, core, hidden_t) + arrived
-    crossed = lax.ppermute(narrow(leaving), "island", other_chip)
-    arrived = lax.ppermute(sums_of(column, 1 - core, hidden_t), "island", other_core)
-    pair = sums_of(column, core, hidden_t) + arrived + widen(crossed).reshape(sums.shape)
+    leaving = call(
+        to_whole,
+        jax.ShapeDtypeStruct(((SIDE + 1) * owners, SIDE), jnp.int16),
+        [vmem, vmem],
+        [pltpu.VMEM((owners, SIDE), f32)],
+        product // 4,
+        "to_whole",
+    )(sums_of(1 - column, core), arrived)
+    crossed = lax.ppermute(leaving, "island", other_chip)
+    arrived = lax.ppermute(sums_of(column, 1 - core, leaving), "island", other_core)
+    pair = sums_of(column, core, leaving) + arrived + from_whole(crossed, owners)
     parts = lax.all_to_all(squeeze(pair), "fsdp", 0, 0, tiled=True)
     total = lax.all_gather(jnp.sum(stretch(parts), axis=0), "island", axis=0)
 

time: 157 us -> 143 us (0.911)
  other arithmetic: 13.5 us -> 6.28 us
  waiting for transfers between devices: 11.6 us -> 9.81 us
    ppermute x2, waiting for transfers between devices: 11.6 us -> 8.19 us  [the longest x1 8.19 us: body(): crossed = lax.ppermute(leaving, 'island', other_chip)]
    convert_element_type x2 -> x0, other arithmetic: 3.11 us -> none  [the longest x1 2.15 us: narrow(): scaled = (values * jnp.exp2(TOP - power)).astype(f16).reshape(-1, SIDE)]
    reduce_max x1 -> x0, other arithmetic: 2.96 us -> none  [narrow(): top = jnp.max(jnp.abs(values))]
    concatenate x2 -> x1, local copies, waits for them, and re-layouts: 1.96 us -> 0.01 us  [body(): payload = jnp.concatenate([own.astype(f32) * TILE_SCALE, meta]).astype(f16)]
    ppermute x1, waiting for transfers between devices: 0.01 us -> 1.62 us  [body(): arrived = lax.ppermute(away, 'island', other_core)]
    pallas_call x3 -> x4, Pallas kernels: 3.95 us -> 4.06 us  [the longest x3 2.99 us: sums_of(): call(kernel, sums, [smem, smem, vmem, vmem] + [far] * len(after), [], 10...]
  transfers between devices with their start and end apart: 4 -> 4, of which waited for: 1 -> 2; matrix products, arithmetic and copies ran while one was open for 6% -> 2% of each run, Pallas kernels for 5% -> 5%
where the time goes in v4:
time: 143 us
  blocking collectives  91.8 us (64%)
  starting transfers between devices  17.9 us (13%)
  Pallas kernels  12.5 us (9%)
  waiting for transfers between devices  9.81 us (7%)
  other arithmetic  6.28 us (4%)
  local copies, waits for them, and re-layouts  3.44 us (2%)
    all_gather x1, blocking collectives, body(): gathered = lax.all_gather(payload, 'fsdp', axis=0)  51.7 us
    all_to_all x1, blocking collectives, body(): parts = lax.all_to_all(squeeze(pair), 'fsdp', 0, 0, tiled=True)  25.9 us
    all_gather x1, blocking collectives, body(): total = lax.all_gather(jnp.sum(stretch(parts), axis=0), 'island', axis=0)  14.2 us
    ppermute x1, starting transfers between devices, body(): theirs = lax.ppermute(mine, 'island', other_core)  8.96 us
    ppermute x1, waiting for transfers between devices, body(): crossed = lax.ppermute(leaving, 'island', other_chip)  8.19 us
    pallas_call x1, Pallas kernels, body(): call(functools.partial(second_matrix, col_blocks, row_blocks), (jax.Shape...  4.92 us
    ppermute x1, starting transfers between devices, body(): crossed = lax.ppermute(leaving, 'island', other_chip)  4.63 us
    pallas_call x1, Pallas kernels, body(): call(functools.partial(first_matrix, col_blocks), blocks, [smem, smem, vm...  3.54 us
  transfers between devices with their start and end apart: 4, of which 2 were waited for; matrix products, arithmetic and copies ran while one was open for 2% of the time, Pallas kernels for 5%

profile of v4, /device:TPU:1, one launch (start us, length us, event | category | flops | bytes accessed | tf_op | source)
XLA Modules:
  0.0 142.6 jit_solution(6974670673980149043)
XLA Ops:
  0.6 0.7 pad_add_fusion
  1.4 1.0 multiply_convert_fusion.1
  2.5 51.7 %all-gather.2 = f16[16,528,128]{2,1,0:T(8,128)(2,1)S(1)} all-gather(f16[1,528,128]{2,1,0:T(8,128)(2,1)S(1)} %pad_maximum_fusion), channel_id=1, replica_groups=mesh['island'=4,'fsdp'=16,'tensor'=16] {'fsdp'}, dimensions={0}, use_global_device_ids=true | all-gather | bytes 2297856 | tf_op jit(solution)/shard_map/all_gather | solution.py:144
  54.2 1.3 copy-done.3
  55.5 1.9 %multiply_convert_fusion.sent = bf16[16,512,128]{2,1,0:T(8,128)(2,1)} fusion(f16[16,528,128]{2,1,0:T(8,128)(2,1)S(1)} %all-gather.2), kind=kLoop, calls=%fused_computation | loop fusion | flops 3145728 | bytes 4194304 | tf_op jit(solution)/shard_map/convert_element_type | solution.py:145
  57.5 9.0 %collective-permute-start = (bf16[16,512,128]{2,1,0:T(8,128)(2,1)}, bf16[16,512,128]{2,1,0:T(8,128)(2,1)}, u32[]{:S(2)}, u32[]{:S(2)}) collective-permute-start(bf16[16,512,128]{2,1,0:T(8,128)(2,1)} %multiply_convert_fusion.sent), channel_id=1, source_target_pairs={{0,256},{256,0},{512,768},{768,512},{1,257},{257,1},{513,769},{769... | collective-permute-start | bytes 6291464 | tf_op jit(solution)/shard_map/ppermute | solution.py:146
  66.5 0.8 slice.16
  67.5 3.5 %first_matrix.1.first = f32[18,256,128]{2,1,0:T(8,128)S(1)} custom-call(s32[16,8]{1,0:T(8,128)S(1)} %copy.17.cells, s32[1]{0:T(128)} %bitcast.8.base, bf16[256,4608]{1,0:T(8,128)(2,1)S(1)} %copy-done, bf16[16,512,128]{2,1,0:T(8,128)(2,1)} %multiply_convert_fusion.sent), custom_call_target="tpu_custom_call" | custom-call | flops 536870912 | bytes 8 | tf_op jit(solution)/shard_map/first_matrix/pallas_call | solution.py:167
  71.0 4.9 %second_matrix.1 = (bf16[2304,256]{1,0:T(8,128)(2,1)S(1)}, f32[16,128,128]{2,1,0:T(8,128)S(1)}) custom-call(s32[16,8]{1,0:T(8,128)S(1)} %copy.17.cells, s32[1]{0:T(128)} %bitcast.6.base, s32[1]{0:T(128)} %bitcast.7.rank, s32[64]{0:T(128)S(1)} %bitcast.47, bf16[16,512,128]{2,1,0:T(8,128)(2,1)} %collective-permute-done.sent, bf16[256,4608]{1,0:T(8,128)(2,1)S(1)} %copy-done, ...), custom_call_target="tpu_custom_call" | custom-call | flops 805306368 | bytes 8 | tf_op jit(solution)/shard_map/second_matrix/pallas_call | solution.py:175
  76.0 1.9 %collective-permute-start.1 = (f32[16,128,128]{2,1,0:T(8,128)S(1)}, f32[16,128,128]{2,1,0:T(8,128)S(1)}, u32[]{:S(2)}, u32[]{:S(2)}) collective-permute-start(f32[16,128,128]{2,1,0:T(8,128)S(1)} %get-tuple-element.5), channel_id=1, source_target_pairs={{0,256},{256,0},{512,768},{768,512},{1,257},{257,1},{513,769},{769... | collective-permute-start | bytes 3145736 | tf_op jit(solution)/shard_map/ppermute | solution.py:184
  77.9 1.0 token_sums.3.ours
  78.9 1.6 %collective-permute-done.1.theirs = f32[16,128,128]{2,1,0:T(8,128)S(1)} collective-permute-done((f32[16,128,128]{2,1,0:T(8,128)S(1)}, f32[16,128,128]{2,1,0:T(8,128)S(1)}, u32[]{:S(2)}, u32[]{:S(2)}) %collective-permute-start.1) | collective-permute-done | bytes 1048608 | tf_op jit(solution)/shard_map/ppermute | solution.py:184
  80.5 1.1 to_whole.1.refs_0_
  81.6 4.6 %collective-permute-start.3 = (s16[2064,128]{1,0:T(8,128)(2,1)}, s16[2064,128]{1,0:T(8,128)(2,1)}, u32[]{:S(2)}, u32[]{:S(2)}) collective-permute-start(s16[2064,128]{1,0:T(8,128)(2,1)} %to_whole.1.refs_0_), channel_id=1, source_target_pairs={{0,512},{256,768},{512,0},{768,256},{1,513},{257,769},{513,1},{769... | collective-permute-start | bytes 1585160 | tf_op jit(solution)/shard_map/ppermute | solution.py:193
  86.2 1.0 token_sums.5
  87.2 2.3 %collective-permute-start.2 = (f32[16,128,128]{2,1,0:T(8,128)S(1)}, f32[16,128,128]{2,1,0:T(8,128)S(1)}, u32[]{:S(2)}, u32[]{:S(2)}) collective-permute-start(f32[16,128,128]{2,1,0:T(8,128)S(1)} %token_sums.5), channel_id=1, source_target_pairs={{0,256},{256,0},{512,768},{768,512},{1,257},{257,1},{513,769},{769... | collective-permute-start | bytes 3145736 | tf_op jit(solution)/shard_map/ppermute | solution.py:194
  89.6 1.0 token_sums.4
  90.6 8.2 %collective-permute-done.3 = s16[2064,128]{1,0:T(8,128)(2,1)} collective-permute-done((s16[2064,128]{1,0:T(8,128)(2,1)}, s16[2064,128]{1,0:T(8,128)(2,1)}, u32[]{:S(2)}, u32[]{:S(2)}) %collective-permute-start.3) | collective-permute-done | bytes 528416 | tf_op jit(solution)/shard_map/ppermute | solution.py:193
  98.8 1.1 slice.18
  99.9 0.7 multiply_exponential_fusion
  100.6 0.7 fusion.2
  101.3 25.9 %all_to_all.5 = f16[16,128,128]{2,1,0:T(8,128)(2,1)S(1)} all-to-all(f16[16,128,128]{2,1,0:T(8,128)(2,1)S(1)} %fusion.2), channel_id=1, replica_groups=mesh['island'=4,'fsdp'=16,'tensor'=16] {'fsdp'}, dimensions={0} | all-to-all | bytes 1048576 | tf_op jit(solution)/shard_map/all_to_all | solution.py:196
  127.4 14.2 %all-gather = f32[512,128]{1,0:T(8,128)S(1)} all-gather(f32[128,128]{1,0:T(8,128)S(1)} %fusion.1), channel_id=2, replica_groups=mesh['island'=4,'fsdp'=16,'tensor'=16] {'island'}, dimensions={0}, use_global_device_ids=true | all-gather | bytes 327680 | tf_op jit(solution)/shard_map/all_gather | solution.py:197
  141.7 0.9 fusion.7
  (21 shorter events, 0.6 us)
Async XLA Ops:
  54.2 1.3 copy-start.3
  55.5 11.9 %copy-start = (bf16[256,4608]{1,0:T(8,128)(2,1)S(1)}, bf16[256,4608]{1,0:T(8,128)(2,1)}, u32[]{:S(2)}) copy-start(bf16[256,4608]{1,0:T(8,128)(2,1)} %tok.3) | copy-start | bytes 7077892
  57.5 13.6 %collective-permute-start = (bf16[16,512,128]{2,1,0:T(8,128)(2,1)}, bf16[16,512,128]{2,1,0:T(8,128)(2,1)}, u32[]{:S(2)}, u32[]{:S(2)}) collective-permute-start(bf16[16,512,128]{2,1,0:T(8,128)(2,1)} %multiply_convert_fusion.sent), channel_id=1, source_target_pairs={{0,256},{256,0},{512,768},{768,512},{1,257},{257,1},{513,769},{769... | collective-permute-start | bytes 6291464 | tf_op jit(solution)/shard_map/ppermute | solution.py:146
  67.5 3.6 %copy-start.1 = (bf16[256,4608]{1,0:T(8,128)(2,1)S(1)}, bf16[256,4608]{1,0:T(8,128)(2,1)}, u32[]{:S(2)}) copy-start(bf16[256,4608]{1,0:T(8,128)(2,1)} %cot.7) | copy-start | bytes 7077892
  67.5 3.6 %copy-start.2 = (s32[64,1]{0,1:T(1,128)S(1)}, s32[64,1]{0,1:T(1,128)}, u32[]{:S(2)}) copy-start(s32[64,1]{0,1:T(1,128)} %param.15) | copy-start | bytes 772
  76.0 4.6 %collective-permute-start.1 = (f32[16,128,128]{2,1,0:T(8,128)S(1)}, f32[16,128,128]{2,1,0:T(8,128)S(1)}, u32[]{:S(2)}, u32[]{:S(2)}) collective-permute-start(f32[16,128,128]{2,1,0:T(8,128)S(1)} %get-tuple-element.5), channel_id=1, source_target_pairs={{0,256},{256,0},{512,768},{768,512},{1,257},{257,1},{513,769},{769... | collective-permute-start | bytes 3145736 | tf_op jit(solution)/shard_map/ppermute | solution.py:184
  81.6 17.2 %collective-permute-start.3 = (s16[2064,128]{1,0:T(8,128)(2,1)}, s16[2064,128]{1,0:T(8,128)(2,1)}, u32[]{:S(2)}, u32[]{:S(2)}) collective-permute-start(s16[2064,128]{1,0:T(8,128)(2,1)} %to_whole.1.refs_0_), channel_id=1, source_target_pairs={{0,512},{256,768},{512,0},{768,256},{1,513},{257,769},{513,1},{769... | collective-permute-start | bytes 1585160 | tf_op jit(solution)/shard_map/ppermute | solution.py:193
  87.2 13.3 %collective-permute-start.2 = (f32[16,128,128]{2,1,0:T(8,128)S(1)}, f32[16,128,128]{2,1,0:T(8,128)S(1)}, u32[]{:S(2)}, u32[]{:S(2)}) collective-permute-start(f32[16,128,128]{2,1,0:T(8,128)S(1)} %token_sums.5), channel_id=1, source_target_pairs={{0,256},{256,0},{512,768},{768,512},{1,257},{257,1},{513,769},{769... | collective-permute-start | bytes 3145736 | tf_op jit(solution)/shard_map/ppermute | solution.py:194
  100.6 41.1 %copy-start.4 = (f32[4,1,128,128]{3,2,1,0:T(8,128)S(1)}, f32[4,1,128,128]{3,2,1,0:T(8,128)}, u32[]{:S(2)}) copy-start(f32[4,1,128,128]{3,2,1,0:T(8,128)} %param.17) | copy-start | bytes 786436
  100.6 41.1 %copy-start.5 = (f32[4,1,128,128]{3,2,1,0:T(8,128)S(1)}, f32[4,1,128,128]{3,2,1,0:T(8,128)}, u32[]{:S(2)}) copy-start(f32[4,1,128,128]{3,2,1,0:T(8,128)} %param.16) | copy-start | bytes 786436

commit v5 on v4

--- a/solution.py
+++ b/solution.py
@@ -9,7 +9,6 @@
 
 FF = 36864
 SIDE = 128
-META = 16
 TILE_SCALE = 2.0**17
 WHOLE = 15.0
 
@@ -27,15 +26,15 @@
     return pl.ds(pl.multiple_of(index * SIDE, SIDE), SIDE)
 
 
-def add_products(col_blocks, cells, base, tok, sent, tiles, sems, acc):
+def add_products(cells, base, tok, sent, tiles, sems, acc):
     owners = cells.shape[0]
-    each = cells.shape[1] // 2
-    together = 8
+    each = cells.shape[1] // 4
+    together = 4
     groups = owners // together
 
     def fetch(group):
         part = pl.ds(group * together, together)
-        return pltpu.make_async_copy(sent.at[part], tiles.at[part], sems.at[group])
+        return pltpu.make_async_copy(sent.at[part, pl.ds(0, each * SIDE)], tiles.at[part], sems.at[group])
 
     for group in range(groups):
         fetch(group).start()
@@ -44,16 +43,15 @@
         fetch(group).wait()
         for owner in range(group * together, (group + 1) * together):
             for k in range(each):
-                cell = cells[owner, base + k]
-                acc[cell % col_blocks] += jnp.dot(
-                    tok[:, block(cell // col_blocks)],
+                acc[cells[owner, 2 * each + base + k]] += jnp.dot(
+                    tok[:, block(cells[owner, base + k])],
                     tiles[owner, k * SIDE:(k + 1) * SIDE, :],
                     preferred_element_type=f32,
                 )
 
 
-def first_matrix(col_blocks, cells, base, tok, sent, acc, tiles, sems):
-    add_products(col_blocks, cells, base[0], tok, sent, tiles, sems, acc)
+def first_matrix(cells, base, tok, sent, acc, tiles, sems):
+    add_products(cells, base[0], tok, sent, tiles, sems, acc)
 
 
 def token_sums(row_blocks, rank, down, hidden_t, cot, *refs):
@@ -66,7 +64,7 @@
 
 
 def second_matrix(col_blocks, row_blocks, cells, base, rank, down, sent, tok, first, cot, hidden_t, out, acc, tiles, sems):
-    add_products(col_blocks, cells, base[0], tok, sent, tiles, sems, acc)
+    add_products(cells, base[0], tok, sent, tiles, sems, acc)
     first_is_gate = base[0] != 0
     together = 6
 
@@ -110,14 +108,14 @@
     out[owners * SIDE:, :] = powers[...].astype(jnp.int32).astype(jnp.int16)
 
 
-def from_whole(sent, owners):
-    scale = jnp.exp2(sent[owners * SIDE:].astype(f32) - WHOLE)
-    return sent[:owners * SIDE].reshape(owners, SIDE, SIDE).astype(f32) * scale[:, None, :]
-
-
-def squeeze(values):
-    root = 0.5 * jnp.sqrt(jnp.abs(values))
-    return jnp.where(values < 0, -root, root).astype(f16)
+def from_whole(ours, theirs, sent, out, scales):
+    owners = ours.shape[0]
+    scales[...] = jnp.exp2(sent[owners * SIDE:, :].astype(jnp.int32).astype(f32) - WHOLE)
+    for z in range(owners):
+        whole = sent[z * SIDE:(z + 1) * SIDE, :].astype(jnp.int32).astype(f32)
+        value = ours[z] + theirs[z] + whole * scales[z:z + 1, :]
+        root = 0.5 * jnp.sqrt(jnp.abs(value))
+        out[z] = jnp.where(value < 0, -root, root)
 
 
 def stretch(sent):
@@ -139,12 +137,13 @@
 
     own = jnp.where(core == 0, gate_tiles, up_tiles).reshape(each * SIDE, SIDE)
     where = jnp.concatenate([gate_where, up_where])
-    meta = jnp.broadcast_to(jnp.pad(where, ((0, META - 2 * each), (0, 0))).astype(f32), (META, SIDE))
+    where = jnp.concatenate([where // col_blocks, where % col_blocks])
+    meta = jnp.broadcast_to(where.astype(f32), (4 * each, SIDE))
     payload = jnp.concatenate([own.astype(f32) * TILE_SCALE, meta]).astype(f16)
     gathered = lax.all_gather(payload, "fsdp", axis=0)
-    mine = (gathered[:, :each * SIDE].astype(f32) * (1.0 / TILE_SCALE)).astype(bf16)
+    mine = (gathered.astype(f32) * (1.0 / TILE_SCALE)).astype(bf16)
+    cells = (mine[:, each * SIDE:, 0].astype(f32) * TILE_SCALE).astype(jnp.int32)
     theirs = lax.ppermute(mine, "island", other_core)
-    cells = gathered[:, each * SIDE:each * SIDE + 2 * each, 0].astype(jnp.int32)
 
     vmem = pl.BlockSpec(memory_space=pltpu.VMEM)
     smem = pl.BlockSpec(memory_space=pltpu.SMEM)
@@ -162,10 +161,10 @@
             rank, down, hidden_t, cotangent, *after
         )
 
-    staged = pltpu.VMEM(mine.shape, bf16)
-    copies = pltpu.SemaphoreType.DMA((owners // 8,))
+    staged = pltpu.VMEM((owners, each * SIDE, SIDE), bf16)
+    copies = pltpu.SemaphoreType.DMA((owners // 4,))
     first = call(
-        functools.partial(first_matrix, col_blocks),
+        first_matrix,
         blocks,
         [smem, smem, vmem, far],
         [staged, copies],
@@ -192,8 +191,10 @@
     )(sums_of(1 - column, core), arrived)
     crossed = lax.ppermute(leaving, "island", other_chip)
     arrived = lax.ppermute(sums_of(column, 1 - core, leaving), "island", other_core)
-    pair = sums_of(column, core, leaving) + arrived + from_whole(crossed, owners)
-    parts = lax.all_to_all(squeeze(pair), "fsdp", 0, 0, tiled=True)
+    roots = call(
+        from_whole, sums, [vmem] * 3, [pltpu.VMEM((owners, SIDE), f32)], product // 4, "from_whole"
+    )(sums_of(column, core, leaving), arrived, crossed)
+    parts = lax.all_to_all(roots.astype(f16), "fsdp", 0, 0, tiled=True)
     total = lax.all_gather(jnp.sum(stretch(parts), axis=0), "island", axis=0)
 
     master = down_global[:, 0]

time: 143 us -> 141 us (0.986)
  local copies, waits for them, and re-layouts: 3.44 us -> 0.04 us
  Pallas kernels: 12.5 us -> 14.4 us
    slice x2 -> x0, local copies, waits for them, and re-layouts: 1.84 us -> none  [the longest x1 1.08 us: from_whole(): sent[:owners * SIDE].reshape(owners, SIDE, SIDE).astype(f32)]
    pallas_call x1 -> x2, Pallas kernels: 3.54 us -> 5.35 us  [the longest x1 3.72 us: body(): call(first_matrix, blocks, [smem, smem, vmem, far], [staged, copies], pro...]
    unnamed x13 -> x10, local copies, waits for them, and re-layouts: 1.51 us -> 0.03 us
  transfers between devices with their start and end apart: 4 -> 4, of which waited for: 2 -> 2; matrix products, arithmetic and copies ran while one was open for 2% -> 1% of each run, Pallas kernels for 5% -> 5%
where the time goes in v5:
time: 141 us
  blocking collectives  91.9 us (65%)
  starting transfers between devices  18 us (13%)
  Pallas kernels  14.4 us (10%)
  waiting for transfers between devices  9.75 us (7%)
  other arithmetic  6.15 us (4%)
    all_gather x1, blocking collectives, body(): gathered = lax.all_gather(payload, 'fsdp', axis=0)  51.7 us
    all_to_all x1, blocking collectives, body(): parts = lax.all_to_all(roots.astype(f16), 'fsdp', 0, 0, tiled=True)  26.1 us
    all_gather x1, blocking collectives, body(): total = lax.all_gather(jnp.sum(stretch(parts), axis=0), 'island', axis=0)  14.2 us
    ppermute x1, starting transfers between devices, body(): theirs = lax.ppermute(mine, 'island', other_core)  9 us
    ppermute x1, waiting for transfers between devices, body(): crossed = lax.ppermute(leaving, 'island', other_chip)  8.16 us
    pallas_call x1, Pallas kernels, body(): call(functools.partial(second_matrix, col_blocks, row_blocks), (jax.Shape...  4.97 us
    ppermute x1, starting transfers between devices, body(): crossed = lax.ppermute(leaving, 'island', other_chip)  4.65 us
    pallas_call x1, Pallas kernels, body(): call(first_matrix, blocks, [smem, smem, vmem, far], [staged, copies], pro...  3.72 us
  transfers between devices with their start and end apart: 4, of which 2 were waited for; matrix products, arithmetic and copies ran while one was open for 1% of the time, Pallas kernels for 5%

profile of v5, /device:TPU:1, one launch (start us, length us, event | category | flops | bytes accessed | tf_op | source)
XLA Modules:
  0.0 141.1 jit_solution(900346389311818506)
XLA Ops:
  0.6 0.8 and_select_fusion.1
  1.5 1.0 multiply_convert_fusion.1
  2.5 0.1 pad_maximum_fusion
  2.6 51.7 %all-gather.2 = f16[16,528,128]{2,1,0:T(8,128)(2,1)S(1)} all-gather(f16[1,528,128]{2,1,0:T(8,128)(2,1)S(1)} %pad_maximum_fusion), channel_id=1, replica_groups=mesh['island'=4,'fsdp'=16,'tensor'=16] {'fsdp'}, dimensions={0}, use_global_device_ids=true | all-gather | bytes 2297856 | tf_op jit(solution)/shard_map/all_gather | solution.py:143
  54.3 1.8 %multiply_convert_fusion.sent = bf16[16,528,128]{2,1,0:T(8,128)(2,1)} fusion(f16[16,528,128]{2,1,0:T(8,128)(2,1)S(1)} %all-gather.2), kind=kLoop, calls=%fused_computation | loop fusion | flops 3244032 | bytes 4325376 | tf_op jit(solution)/shard_map/convert_element_type | solution.py:144
  56.1 9.0 %collective-permute-start = (bf16[16,528,128]{2,1,0:T(8,128)(2,1)}, bf16[16,528,128]{2,1,0:T(8,128)(2,1)}, u32[]{:S(2)}, u32[]{:S(2)}) collective-permute-start(bf16[16,528,128]{2,1,0:T(8,128)(2,1)} %multiply_convert_fusion.sent), channel_id=1, source_target_pairs={{0,256},{256,0},{512,768},{768,512},{1,257},{257,1},{513,769},{769... | collective-permute-start | bytes 6488072 | tf_op jit(solution)/shard_map/ppermute | solution.py:146
  65.1 1.2 convert_reduce_fusion.cells
  66.4 3.7 %first_matrix.1.first = f32[18,256,128]{2,1,0:T(8,128)S(1)} custom-call(s32[16,16]{1,0:T(8,128)S(1)} %convert_reduce_fusion.cells, s32[1]{0:T(128)} %bitcast.8.base, bf16[256,4608]{1,0:T(8,128)(2,1)S(1)} %copy-done, bf16[16,528,128]{2,1,0:T(8,128)(2,1)} %multiply_convert_fusion.sent), custom_call_target="tpu_custom_call" | custom-call | flops 536870912 | bytes 8 | tf_op jit(solution)/shard_map/first_matrix/pallas_call | solution.py:166
  70.1 5.0 %second_matrix.1 = (bf16[2304,256]{1,0:T(8,128)(2,1)S(1)}, f32[16,128,128]{2,1,0:T(8,128)S(1)}) custom-call(s32[16,16]{1,0:T(8,128)S(1)} %convert_reduce_fusion.cells, s32[1]{0:T(128)} %bitcast.6.base, s32[1]{0:T(128)} %bitcast.7.rank, s32[64]{0:T(128)S(1)} %bitcast.42, bf16[16,528,128]{2,1,0:T(8,128)(2,1)} %collective-permute-done.sent, ...), custom_call_target="tpu_custom_call" | custom-call | flops 805306368 | bytes 8 | tf_op jit(solution)/shard_map/second_matrix/pallas_call | solution.py:174
  75.1 2.0 %collective-permute-start.1 = (f32[16,128,128]{2,1,0:T(8,128)S(1)}, f32[16,128,128]{2,1,0:T(8,128)S(1)}, u32[]{:S(2)}, u32[]{:S(2)}) collective-permute-start(f32[16,128,128]{2,1,0:T(8,128)S(1)} %get-tuple-element.5), channel_id=1, source_target_pairs={{0,256},{256,0},{512,768},{768,512},{1,257},{257,1},{513,769},{769... | collective-permute-start | bytes 3145736 | tf_op jit(solution)/shard_map/ppermute | solution.py:183
  77.1 1.0 token_sums.3.ours
  78.1 1.6 %collective-permute-done.1.theirs = f32[16,128,128]{2,1,0:T(8,128)S(1)} collective-permute-done((f32[16,128,128]{2,1,0:T(8,128)S(1)}, f32[16,128,128]{2,1,0:T(8,128)S(1)}, u32[]{:S(2)}, u32[]{:S(2)}) %collective-permute-start.1) | collective-permute-done | bytes 1048608 | tf_op jit(solution)/shard_map/ppermute | solution.py:183
  79.7 1.1 to_whole.1.refs_0_
  80.7 4.7 %collective-permute-start.3 = (s16[2064,128]{1,0:T(8,128)(2,1)}, s16[2064,128]{1,0:T(8,128)(2,1)}, u32[]{:S(2)}, u32[]{:S(2)}) collective-permute-start(s16[2064,128]{1,0:T(8,128)(2,1)} %to_whole.1.refs_0_), channel_id=1, source_target_pairs={{0,512},{256,768},{512,0},{768,256},{1,513},{257,769},{513,1},{769... | collective-permute-start | bytes 1585160 | tf_op jit(solution)/shard_map/ppermute | solution.py:192
  85.4 1.0 token_sums.5
  86.4 2.3 %collective-permute-start.2 = (f32[16,128,128]{2,1,0:T(8,128)S(1)}, f32[16,128,128]{2,1,0:T(8,128)S(1)}, u32[]{:S(2)}, u32[]{:S(2)}) collective-permute-start(f32[16,128,128]{2,1,0:T(8,128)S(1)} %token_sums.5), channel_id=1, source_target_pairs={{0,256},{256,0},{512,768},{768,512},{1,257},{257,1},{513,769},{769... | collective-permute-start | bytes 3145736 | tf_op jit(solution)/shard_map/ppermute | solution.py:193
  88.7 1.0 token_sums.4.ours
  89.7 8.2 %collective-permute-done.3.sent = s16[2064,128]{1,0:T(8,128)(2,1)} collective-permute-done((s16[2064,128]{1,0:T(8,128)(2,1)}, s16[2064,128]{1,0:T(8,128)(2,1)}, u32[]{:S(2)}, u32[]{:S(2)}) %collective-permute-start.3) | collective-permute-done | bytes 528416 | tf_op jit(solution)/shard_map/ppermute | solution.py:192
  97.9 1.6 %from_whole.1 = f32[16,128,128]{2,1,0:T(8,128)S(1)} custom-call(f32[16,128,128]{2,1,0:T(8,128)S(1)} %token_sums.4.ours, f32[16,128,128]{2,1,0:T(8,128)S(1)} %collective-permute-done.2.theirs, s16[2064,128]{1,0:T(8,128)(2,1)} %collective-permute-done.3.sent), custom_call_target="tpu_custom_call" | custom-call | flops 134217728 | bytes 8 | tf_op jit(solution)/shard_map/from_whole/pallas_call | solution.py:194
  99.6 0.1 convert_element_type.54
  99.7 26.1 %all_to_all.5 = f16[16,128,128]{2,1,0:T(8,128)(2,1)S(1)} all-to-all(f16[16,128,128]{2,1,0:T(8,128)(2,1)S(1)} %convert_element_type.54), channel_id=1, replica_groups=mesh['island'=4,'fsdp'=16,'tensor'=16] {'fsdp'}, dimensions={0} | all-to-all | bytes 1048576 | tf_op jit(solution)/shard_map/all_to_all | solution.py:197
  125.7 0.2 fusion.1
  125.9 14.2 %all-gather = f32[512,128]{1,0:T(8,128)S(1)} all-gather(f32[128,128]{1,0:T(8,128)S(1)} %fusion.1), channel_id=2, replica_groups=mesh['island'=4,'fsdp'=16,'tensor'=16] {'island'}, dimensions={0}, use_global_device_ids=true | all-gather | bytes 327680 | tf_op jit(solution)/shard_map/all_gather | solution.py:198
  140.2 0.9 fusion.5
  (15 shorter events, 0.1 us)
Async XLA Ops:
  54.3 12.1 %copy-start = (bf16[256,4608]{1,0:T(8,128)(2,1)S(1)}, bf16[256,4608]{1,0:T(8,128)(2,1)}, u32[]{:S(2)}) copy-start(bf16[256,4608]{1,0:T(8,128)(2,1)} %tok.3) | copy-start | bytes 7077892
  56.1 14.0 %collective-permute-start = (bf16[16,528,128]{2,1,0:T(8,128)(2,1)}, bf16[16,528,128]{2,1,0:T(8,128)(2,1)}, u32[]{:S(2)}, u32[]{:S(2)}) collective-permute-start(bf16[16,528,128]{2,1,0:T(8,128)(2,1)} %multiply_convert_fusion.sent), channel_id=1, source_target_pairs={{0,256},{256,0},{512,768},{768,512},{1,257},{257,1},{513,769},{769... | collective-permute-start | bytes 6488072 | tf_op jit(solution)/shard_map/ppermute | solution.py:146
  66.3 3.8 %copy-start.1 = (bf16[256,4608]{1,0:T(8,128)(2,1)S(1)}, bf16[256,4608]{1,0:T(8,128)(2,1)}, u32[]{:S(2)}) copy-start(bf16[256,4608]{1,0:T(8,128)(2,1)} %cot.7) | copy-start | bytes 7077892
  66.3 3.8 %copy-start.2 = (s32[64,1]{0,1:T(1,128)S(1)}, s32[64,1]{0,1:T(1,128)}, u32[]{:S(2)}) copy-start(s32[64,1]{0,1:T(1,128)} %param.15) | copy-start | bytes 772
  75.1 4.6 %collective-permute-start.1 = (f32[16,128,128]{2,1,0:T(8,128)S(1)}, f32[16,128,128]{2,1,0:T(8,128)S(1)}, u32[]{:S(2)}, u32[]{:S(2)}) collective-permute-start(f32[16,128,128]{2,1,0:T(8,128)S(1)} %get-tuple-element.5), channel_id=1, source_target_pairs={{0,256},{256,0},{512,768},{768,512},{1,257},{257,1},{513,769},{769... | collective-permute-start | bytes 3145736 | tf_op jit(solution)/shard_map/ppermute | solution.py:183
  80.7 17.2 %collective-permute-start.3 = (s16[2064,128]{1,0:T(8,128)(2,1)}, s16[2064,128]{1,0:T(8,128)(2,1)}, u32[]{:S(2)}, u32[]{:S(2)}) collective-permute-start(s16[2064,128]{1,0:T(8,128)(2,1)} %to_whole.1.refs_0_), channel_id=1, source_target_pairs={{0,512},{256,768},{512,0},{768,256},{1,513},{257,769},{513,1},{769... | collective-permute-start | bytes 1585160 | tf_op jit(solution)/shard_map/ppermute | solution.py:192
  86.4 11.5 %collective-permute-start.2 = (f32[16,128,128]{2,1,0:T(8,128)S(1)}, f32[16,128,128]{2,1,0:T(8,128)S(1)}, u32[]{:S(2)}, u32[]{:S(2)}) collective-permute-start(f32[16,128,128]{2,1,0:T(8,128)S(1)} %token_sums.5), channel_id=1, source_target_pairs={{0,256},{256,0},{512,768},{768,512},{1,257},{257,1},{513,769},{769... | collective-permute-start | bytes 3145736 | tf_op jit(solution)/shard_map/ppermute | solution.py:193
  99.5 40.6 %copy-start.3 = (f32[4,1,128,128]{3,2,1,0:T(8,128)S(1)}, f32[4,1,128,128]{3,2,1,0:T(8,128)}, u32[]{:S(2)}) copy-start(f32[4,1,128,128]{3,2,1,0:T(8,128)} %param.17) | copy-start | bytes 786436
  99.5 40.6 %copy-start.4 = (f32[4,1,128,128]{3,2,1,0:T(8,128)S(1)}, f32[4,1,128,128]{3,2,1,0:T(8,128)}, u32[]{:S(2)}) copy-start(f32[4,1,128,128]{3,2,1,0:T(8,128)} %param.16) | copy-start | bytes 786436

commit v6 on v5

--- a/solution.py
+++ b/solution.py
@@ -54,16 +54,17 @@
     add_products(cells, base[0], tok, sent, tiles, sems, acc)
 
 
-def token_sums(row_blocks, rank, down, hidden_t, cot, *refs):
-    out = refs[-1]
-    for z in range(out.shape[0]):
-        place = down[z * 4 + rank[0]]
-        out[z] = jnp.dot(
-            hidden_t[block(place // row_blocks), :], cot[:, block(place % row_blocks)], preferred_element_type=f32
-        )
-
-
-def second_matrix(col_blocks, row_blocks, cells, base, rank, down, sent, tok, first, cot, hidden_t, out, acc, tiles, sems):
+def token_sums(row_blocks, side, down, hidden_t, cot, out):
+    columns, owners = out.shape[:2]
+    for h in range(columns):
+        for z in range(owners):
+            place = down[z * 4 + h * 2 + side[0]]
+            out[h, z] = jnp.dot(
+                hidden_t[block(place // row_blocks), :], cot[:, block(place % row_blocks)], preferred_element_type=f32
+            )
+
+
+def second_matrix(col_blocks, row_blocks, cells, base, side, down, sent, tok, first, cot, hidden_t, out, acc, tiles, sems):
     add_products(cells, base[0], tok, sent, tiles, sems, acc)
     first_is_gate = base[0] != 0
     together = 6
@@ -79,7 +80,7 @@
         return carry
 
     lax.fori_loop(0, col_blocks // together, activate, 0)
-    token_sums(row_blocks, rank, down, hidden_t, cot, out)
+    token_sums(row_blocks, side, down, hidden_t, cot, out)
 
 
 def call(kernel, out_shape, in_specs, scratch, flops, name):
@@ -97,30 +98,38 @@
 
 
 def to_whole(ours, theirs, out, powers):
-    owners = ours.shape[0]
+    columns, owners = ours.shape[:2]
+    half = SIDE // 2
+    for h in range(columns):
+        for b in range(2):
+            chunk = 2 * h + b
+            for z in range(owners):
+                rows = slice(b * half, (b + 1) * half)
+                value = ours[h, z, rows, :] + theirs[h, z, rows, :]
+                top = jnp.max(jnp.abs(value), axis=0, keepdims=True)
+                power = jnp.floor(jnp.log2(jnp.maximum(top, 1e-30))) + 1.0
+                whole = jnp.clip(jnp.round(value * jnp.exp2(WHOLE - power)), -32767.0, 32767.0)
+                out[chunk, z * half:(z + 1) * half, :] = whole.astype(jnp.int32).astype(jnp.int16)
+                powers[z:z + 1, :] = power
+            out[chunk, owners * half:, :] = powers[...].astype(jnp.int32).astype(jnp.int16)
+
+
+def from_whole(sent, out, scales):
+    chunks = sent.shape[0]
+    owners, half = out.shape[:2]
+    for k in range(chunks):
+        scales[k] = jnp.exp2(sent[k, owners * half:, :].astype(jnp.int32).astype(f32) - WHOLE)
     for z in range(owners):
-        value = ours[z] + theirs[z]
-        top = jnp.max(jnp.abs(value), axis=0, keepdims=True)
-        power = jnp.floor(jnp.log2(jnp.maximum(top, 1e-30))) + 1.0
-        whole = jnp.round(value * jnp.exp2(WHOLE - power))
-        out[z * SIDE:(z + 1) * SIDE, :] = jnp.clip(whole, -32767.0, 32767.0).astype(jnp.int32).astype(jnp.int16)
-        powers[z:z + 1, :] = power
-    out[owners * SIDE:, :] = powers[...].astype(jnp.int32).astype(jnp.int16)
-
-
-def from_whole(ours, theirs, sent, out, scales):
-    owners = ours.shape[0]
-    scales[...] = jnp.exp2(sent[owners * SIDE:, :].astype(jnp.int32).astype(f32) - WHOLE)
-    for z in range(owners):
-        whole = sent[z * SIDE:(z + 1) * SIDE, :].astype(jnp.int32).astype(f32)
-        value = ours[z] + theirs[z] + whole * scales[z:z + 1, :]
-        root = 0.5 * jnp.sqrt(jnp.abs(value))
+        value = jnp.zeros((half, SIDE), f32)
+        for k in range(chunks):
+            value += sent[k, z * half:(z + 1) * half, :].astype(jnp.int32).astype(f32) * scales[k, z:z + 1, :]
+        root = 0.25 * jnp.sqrt(jnp.abs(value))
         out[z] = jnp.where(value < 0, -root, root)
 
 
 def stretch(sent):
     root = sent.astype(f32)
-    return 4.0 * root * jnp.abs(root)
+    return 16.0 * root * jnp.abs(root)
 
 
 def body(tokens, cotangent, gate_tiles, up_tiles, gate_where, up_where, down_where, down_global, down_moment):
@@ -131,9 +140,11 @@
     owners = lax.axis_size("fsdp")
     islands = lax.axis_size("island")
     me = lax.axis_index("island")
-    core, column = me % 2, me // 2
+    core = me % 2
     other_core = [(i, i ^ 1) for i in range(islands)]
-    other_chip = [(i, i ^ 2) for i in range(islands)]
+    fours = [
+        [(2 * h + c) * owners + 2 * q + b for h in range(2) for b in range(2)] for c in range(2) for q in range(owners // 2)
+    ]
 
     own = jnp.where(core == 0, gate_tiles, up_tiles).reshape(each * SIDE, SIDE)
     where = jnp.concatenate([gate_where, up_where])
@@ -149,17 +160,10 @@
     smem = pl.BlockSpec(memory_space=pltpu.SMEM)
     far = pl.BlockSpec(memory_space=pl.ANY)
     blocks = jax.ShapeDtypeStruct((col_blocks, count, SIDE), f32)
-    sums = jax.ShapeDtypeStruct((owners, SIDE, SIDE), f32)
+    sums = jax.ShapeDtypeStruct((2, owners, SIDE, SIDE), f32)
     kept = each * owners
     down = down_where[:, 0]
     product = 2 * kept * count * SIDE * SIDE
-
-    def sums_of(chip, side, *after):
-        kernel = functools.partial(token_sums, row_blocks)
-        rank = (chip * 2 + side)[None]
-        return call(kernel, sums, [smem, smem, vmem, vmem] + [far] * len(after), [], 10**11, "token_sums")(
-            rank, down, hidden_t, cotangent, *after
-        )
 
     staged = pltpu.VMEM((owners, each * SIDE, SIDE), bf16)
     copies = pltpu.SemaphoreType.DMA((owners // 4,))
@@ -178,24 +182,33 @@
         [pltpu.VMEM(blocks.shape, f32), staged, copies],
         product * 3 // 2,
         "second_matrix",
-    )(cells, ((1 - core) * each)[None], ((1 - column) * 2 + 1 - core)[None], down, theirs, tokens, first, cotangent)
+    )(cells, ((1 - core) * each)[None], (1 - core)[None], down, theirs, tokens, first, cotangent)
 
     arrived = lax.ppermute(away, "island", other_core)
+    stay = call(
+        functools.partial(token_sums, row_blocks), sums, [smem, smem, vmem, vmem], [], 10**11, "token_sums"
+    )(core[None], down, hidden_t, cotangent)
+    half = SIDE // 2
     leaving = call(
         to_whole,
-        jax.ShapeDtypeStruct(((SIDE + 1) * owners, SIDE), jnp.int16),
+        jax.ShapeDtypeStruct((4, (half + 1) * owners, SIDE), jnp.int16),
         [vmem, vmem],
         [pltpu.VMEM((owners, SIDE), f32)],
         product // 4,
         "to_whole",
-    )(sums_of(1 - column, core), arrived)
-    crossed = lax.ppermute(leaving, "island", other_chip)
-    arrived = lax.ppermute(sums_of(column, 1 - core, leaving), "island", other_core)
+    )(stay, arrived)
+    crossed = lax.all_to_all(leaving, ("island", "fsdp"), 0, 0, tiled=True, axis_index_groups=fours)
     roots = call(
-        from_whole, sums, [vmem] * 3, [pltpu.VMEM((owners, SIDE), f32)], product // 4, "from_whole"
-    )(sums_of(column, core, leaving), arrived, crossed)
+        from_whole,
+        jax.ShapeDtypeStruct((owners, half, SIDE), f32),
+        [vmem],
+        [pltpu.VMEM((4, owners, SIDE), f32)],
+        product // 4,
+        "from_whole",
+    )(crossed)
     parts = lax.all_to_all(roots.astype(f16), "fsdp", 0, 0, tiled=True)
-    total = lax.all_gather(jnp.sum(stretch(parts), axis=0), "island", axis=0)
+    tile = jnp.sum(stretch(parts).reshape(owners // 2, 2, half, SIDE), axis=0).reshape(SIDE, SIDE)
+    total = lax.all_gather(tile, "island", axis=0)
 
     master = down_global[:, 0]
     moment = down_moment[:, 0]

time: 141 us -> 133 us (0.943)
  blocking collectives: 91.9 us -> 101 us
  starting transfers between devices: 18 us -> 10.9 us
  waiting for transfers between devices: 9.75 us -> 2.83 us
  Pallas kernels: 14.4 us -> 11.3 us
    all_to_all x0 -> x1, blocking collectives: none -> 19.3 us  [body(): lax.all_to_all(leaving, ('island', 'fsdp'), 0, 0, tiled=True, axis_index_...]
    all_to_all x1, blocking collectives: 26.1 us -> 16.2 us  [body(): parts = lax.all_to_all(roots.astype(f16), 'fsdp', 0, 0, tiled=True)]
    ppermute x2 -> x0, waiting for transfers between devices: 8.16 us -> none  [the longest x1 8.16 us: body(): crossed = lax.ppermute(leaving, 'island', other_chip)]
    ppermute x2 -> x0, starting transfers between devices: 6.99 us -> none  [the longest x1 4.65 us: body(): crossed = lax.ppermute(leaving, 'island', other_chip)]
    pallas_call x5 -> x3, Pallas kernels: 5.68 us -> 2.33 us  [the longest x1 1.28 us: body(): call(functools.partial(token_sums, row_blocks), sums, [smem, smem, vmem,...]
  transfers between devices with their start and end apart: 4 -> 2, of which waited for: 2 -> 1; matrix products, arithmetic and copies ran while one was open for 1% -> 1% of each run, Pallas kernels for 5% -> 4%
where the time goes in v6:
time: 133 us
  blocking collectives  101 us (76%)
  Pallas kernels  11.3 us (8%)
  starting transfers between devices  10.9 us (8%)
  other arithmetic  6.02 us (5%)
  waiting for transfers between devices  2.83 us (2%)
    all_gather x1, blocking collectives, body(): gathered = lax.all_gather(payload, 'fsdp', axis=0)  51.7 us
    all_to_all x1, blocking collectives, body(): lax.all_to_all(leaving, ('island', 'fsdp'), 0, 0, tiled=True, axis_index_...  19.3 us
    all_to_all x1, blocking collectives, body(): parts = lax.all_to_all(roots.astype(f16), 'fsdp', 0, 0, tiled=True)  16.2 us
    all_gather x1, blocking collectives, body(): total = lax.all_gather(tile, 'island', axis=0)  13.9 us
    ppermute x1, starting transfers between devices, body(): theirs = lax.ppermute(mine, 'island', other_core)  9 us
    pallas_call x1, Pallas kernels, body(): call(functools.partial(second_matrix, col_blocks, row_blocks), (jax.Shape...  5.28 us
    pallas_call x1, Pallas kernels, body(): call(first_matrix, blocks, [smem, smem, vmem, far], [staged, copies], pro...  3.72 us
    ppermute x1, waiting for transfers between devices, body(): arrived = lax.ppermute(away, 'island', other_core)  2.82 us
  transfers between devices with their start and end apart: 2, of which 1 were waited for; matrix products, arithmetic and copies ran while one was open for 1% of the time, Pallas kernels for 4%

profile of v6, /device:TPU:1, one launch (start us, length us, event | category | flops | bytes accessed | tf_op | source)
XLA Modules:
  0.0 132.9 jit_solution(14611743248643588682)
XLA Ops:
  0.6 0.8 and_select_fusion.1
  1.4 0.1 fusion.5
  1.5 1.0 multiply_convert_fusion.1
  2.5 0.1 pad_maximum_fusion
  2.6 51.7 %all-gather.1 = f16[16,528,128]{2,1,0:T(8,128)(2,1)S(1)} all-gather(f16[1,528,128]{2,1,0:T(8,128)(2,1)S(1)} %pad_maximum_fusion), channel_id=1, replica_groups=mesh['island'=4,'fsdp'=16,'tensor'=16] {'fsdp'}, dimensions={0}, use_global_device_ids=true | all-gather | bytes 2297856 | tf_op jit(solution)/shard_map/all_gather | solution.py:154
  54.3 1.9 %multiply_convert_fusion.sent = bf16[16,528,128]{2,1,0:T(8,128)(2,1)} fusion(f16[16,528,128]{2,1,0:T(8,128)(2,1)S(1)} %all-gather.1), kind=kLoop, calls=%fused_computation | loop fusion | flops 3244032 | bytes 4325376 | tf_op jit(solution)/shard_map/convert_element_type | solution.py:155
  56.1 9.0 %collective-permute-start = (bf16[16,528,128]{2,1,0:T(8,128)(2,1)}, bf16[16,528,128]{2,1,0:T(8,128)(2,1)}, u32[]{:S(2)}, u32[]{:S(2)}) collective-permute-start(bf16[16,528,128]{2,1,0:T(8,128)(2,1)} %multiply_convert_fusion.sent), channel_id=1, source_target_pairs={{0,256},{256,0},{512,768},{768,512},{1,257},{257,1},{513,769},{769... | collective-permute-start | bytes 6488072 | tf_op jit(solution)/shard_map/ppermute | solution.py:157
  65.1 1.2 convert_reduce_fusion.cells
  66.3 0.0 copy-start.1
  66.3 0.0 copy-start.2
  66.3 3.7 %first_matrix.1.first = f32[18,256,128]{2,1,0:T(8,128)S(1)} custom-call(s32[16,16]{1,0:T(8,128)S(1)} %convert_reduce_fusion.cells, s32[1]{0:T(128)} %bitcast.8.base, bf16[256,4608]{1,0:T(8,128)(2,1)S(1)} %copy-done, bf16[16,528,128]{2,1,0:T(8,128)(2,1)} %multiply_convert_fusion.sent), custom_call_target="tpu_custom_call" | custom-call | flops 536870912 | bytes 8 | tf_op jit(solution)/shard_map/first_matrix/pallas_call | solution.py:170
  70.1 0.0 collective-permute-done.sent
  70.1 5.3 %second_matrix.1 = (bf16[2304,256]{1,0:T(8,128)(2,1)S(1)}, f32[2,16,128,128]{3,2,1,0:T(8,128)S(1)}) custom-call(s32[16,16]{1,0:T(8,128)S(1)} %convert_reduce_fusion.cells, s32[1]{0:T(128)} %bitcast.6.base, s32[1]{0:T(128)} %bitcast.7.side, s32[64]{0:T(128)S(1)} %bitcast.49, bf16[16,528,128]{2,1,0:T(8,128)(2,1)} %collective-permute-done.sent, ...), custom_call_target="tpu_custom_call" | custom-call | flops 805306368 | bytes 8 | tf_op jit(solution)/shard_map/second_matrix/pallas_call | solution.py:178
  75.4 1.9 %collective-permute-start.1 = (f32[2,16,128,128]{3,2,1,0:T(8,128)S(1)}, f32[2,16,128,128]{3,2,1,0:T(8,128)S(1)}, u32[]{:S(2)}, u32[]{:S(2)}) collective-permute-start(f32[2,16,128,128]{3,2,1,0:T(8,128)S(1)} %get-tuple-element.5), channel_id=1, source_target_pairs={{0,256},{256,0},{512,768},{768,512},{1,257},{257,1},{513,769},{769... | collective-permute-start | bytes 6291464 | tf_op jit(solution)/shard_map/ppermute | solution.py:187
  77.3 1.3 token_sums.1.ours
  78.6 2.8 %collective-permute-done.1.theirs = f32[2,16,128,128]{3,2,1,0:T(8,128)S(1)} collective-permute-done((f32[2,16,128,128]{3,2,1,0:T(8,128)S(1)}, f32[2,16,128,128]{3,2,1,0:T(8,128)S(1)}, u32[]{:S(2)}, u32[]{:S(2)}) %collective-permute-start.1) | collective-permute-done | bytes 2097184 | tf_op jit(solution)/shard_map/ppermute | solution.py:187
  81.5 0.6 to_whole.1
  82.0 19.3 %all_to_all.10.sent = s16[4,1040,128]{2,1,0:T(8,128)(2,1)S(1)} all-to-all(s16[4,1040,128]{2,1,0:T(8,128)(2,1)S(1)} %to_whole.1), channel_id=1, replica_groups={{0,16,512,528},{32,48,544,560},{64,80,576,592},{96,112,608,624},{128,14..., dimensions={0} | all-to-all | bytes 2129920 | tf_op jit(solution)/shard_map/all_to_all | solution.py:200
  101.3 0.5 from_whole.1
  101.8 16.2 %all_to_all.11 = f16[16,64,128]{2,1,0:T(8,128)(2,1)S(1)} all-to-all(f16[16,64,128]{2,1,0:T(8,128)(2,1)S(1)} %convert_element_type.54), channel_id=1, replica_groups=mesh['island'=4,'fsdp'=16,'tensor'=16] {'fsdp'}, dimensions={0} | all-to-all | bytes 524288 | tf_op jit(solution)/shard_map/all_to_all | solution.py:209
  118.0 0.1 fusion
  118.1 13.9 %all_gather.8 = f32[4,128,128]{2,1,0:T(8,128)S(1)} all-gather(f32[1,128,128]{2,1,0:T(8,128)S(1)} %bitcast.53), channel_id=1, replica_groups=mesh['island'=4,'fsdp'=16,'tensor'=16] {'island'}, dimensions={0}, use_global_device_ids=true | all-gather | bytes 327680 | tf_op jit(solution)/shard_map/all_gather | solution.py:211
  132.0 0.0 copy-done.3
  132.0 0.9 fusion.4
  (10 shorter events, 0.1 us)
Async XLA Ops:
  54.3 12.1 %copy-start = (bf16[256,4608]{1,0:T(8,128)(2,1)S(1)}, bf16[256,4608]{1,0:T(8,128)(2,1)}, u32[]{:S(2)}) copy-start(bf16[256,4608]{1,0:T(8,128)(2,1)} %tok.3) | copy-start | bytes 7077892
  56.1 14.0 %collective-permute-start = (bf16[16,528,128]{2,1,0:T(8,128)(2,1)}, bf16[16,528,128]{2,1,0:T(8,128)(2,1)}, u32[]{:S(2)}, u32[]{:S(2)}) collective-permute-start(bf16[16,528,128]{2,1,0:T(8,128)(2,1)} %multiply_convert_fusion.sent), channel_id=1, source_target_pairs={{0,256},{256,0},{512,768},{768,512},{1,257},{257,1},{513,769},{769... | collective-permute-start | bytes 6488072 | tf_op jit(solution)/shard_map/ppermute | solution.py:157
  66.3 3.8 %copy-start.1 = (bf16[256,4608]{1,0:T(8,128)(2,1)S(1)}, bf16[256,4608]{1,0:T(8,128)(2,1)}, u32[]{:S(2)}) copy-start(bf16[256,4608]{1,0:T(8,128)(2,1)} %cot.3) | copy-start | bytes 7077892
  66.3 3.8 %copy-start.2 = (s32[64,1]{0,1:T(1,128)S(1)}, s32[64,1]{0,1:T(1,128)}, u32[]{:S(2)}) copy-start(s32[64,1]{0,1:T(1,128)} %param.15) | copy-start | bytes 772
  75.4 6.1 %collective-permute-start.1 = (f32[2,16,128,128]{3,2,1,0:T(8,128)S(1)}, f32[2,16,128,128]{3,2,1,0:T(8,128)S(1)}, u32[]{:S(2)}, u32[]{:S(2)}) collective-permute-start(f32[2,16,128,128]{3,2,1,0:T(8,128)S(1)} %get-tuple-element.5), channel_id=1, source_target_pairs={{0,256},{256,0},{512,768},{768,512},{1,257},{257,1},{513,769},{769... | collective-permute-start | bytes 6291464 | tf_op jit(solution)/shard_map/ppermute | solution.py:187
  101.3 30.7 %copy-start.3 = (f32[4,1,128,128]{3,2,1,0:T(8,128)S(1)}, f32[4,1,128,128]{3,2,1,0:T(8,128)}, u32[]{:S(2)}) copy-start(f32[4,1,128,128]{3,2,1,0:T(8,128)} %param.16) | copy-start | bytes 786436
  101.3 30.7 %copy-start.4 = (f32[4,1,128,128]{3,2,1,0:T(8,128)S(1)}, f32[4,1,128,128]{3,2,1,0:T(8,128)}, u32[]{:S(2)}) copy-start(f32[4,1,128,128]{3,2,1,0:T(8,128)} %param.17) | copy-start | bytes 786436

commit v7 on v6

--- a/solution.py
+++ b/solution.py
@@ -11,6 +11,7 @@
 SIDE = 128
 TILE_SCALE = 2.0**17
 WHOLE = 15.0
+MARK = 16
 
 inner_rate = 0.5
 decay_rate = 0.1
@@ -20,6 +21,7 @@
 f32 = jnp.float32
 bf16 = jnp.bfloat16
 f16 = jnp.float16
+s16 = jnp.int16
 
 
 def block(index):
@@ -54,17 +56,37 @@
     add_products(cells, base[0], tok, sent, tiles, sems, acc)
 
 
-def token_sums(row_blocks, side, down, hidden_t, cot, out):
+def to_whole(value):
+    top = jnp.max(jnp.abs(value), axis=0, keepdims=True)
+    power = jnp.floor(jnp.log2(jnp.maximum(top, 1e-30))) + 1.0
+    whole = jnp.clip(jnp.round(value * jnp.exp2(WHOLE - power)), -32767.0, 32767.0)
+    return whole.astype(jnp.int32).astype(s16), power
+
+
+def wide(whole):
+    return whole.astype(jnp.int32).astype(f32)
+
+
+def scale_of(powers):
+    return jnp.exp2(wide(powers) - WHOLE)
+
+
+def token_sum(row_blocks, place, hidden_t, cot):
+    return jnp.dot(
+        hidden_t[block(place // row_blocks), :], cot[:, block(place % row_blocks)], preferred_element_type=f32
+    )
+
+
+def keep_sums(row_blocks, side, down, hidden_t, cot, out):
     columns, owners = out.shape[:2]
     for h in range(columns):
         for z in range(owners):
-            place = down[z * 4 + h * 2 + side[0]]
-            out[h, z] = jnp.dot(
-                hidden_t[block(place // row_blocks), :], cot[:, block(place % row_blocks)], preferred_element_type=f32
-            )
-
-
-def second_matrix(col_blocks, row_blocks, cells, base, side, down, sent, tok, first, cot, hidden_t, out, acc, tiles, sems):
+            out[h, z] = token_sum(row_blocks, down[z * 4 + h * 2 + side[0]], hidden_t, cot)
+
+
+def second_matrix(
+    col_blocks, row_blocks, cells, base, side, down, sent, tok, first, cot, hidden_t, out, acc, tiles, sems, powers
+):
     add_products(cells, base[0], tok, sent, tiles, sems, acc)
     first_is_gate = base[0] != 0
     together = 6
@@ -80,7 +102,14 @@
         return carry
 
     lax.fori_loop(0, col_blocks // together, activate, 0)
-    token_sums(row_blocks, side, down, hidden_t, cot, out)
+    count = powers.shape[0]
+    owners = count // 2
+    for t in range(count):
+        place = down[t % owners * 4 + t // owners * 2 + side[0]]
+        whole, power = to_whole(token_sum(row_blocks, place, hidden_t, cot))
+        out[t * SIDE:(t + 1) * SIDE, :] = whole
+        powers[t:t + 1, :] = power
+    out[count * SIDE:, :] = powers[...].astype(jnp.int32).astype(s16)
 
 
 def call(kernel, out_shape, in_specs, scratch, flops, name):
@@ -97,39 +126,46 @@
     )
 
 
-def to_whole(ours, theirs, out, powers):
+def add_cores(ours, theirs, out, scales, powers):
     columns, owners = ours.shape[:2]
     half = SIDE // 2
+    scales[...] = scale_of(theirs[columns * owners * SIDE:, :])
     for h in range(columns):
         for b in range(2):
             chunk = 2 * h + b
             for z in range(owners):
-                rows = slice(b * half, (b + 1) * half)
-                value = ours[h, z, rows, :] + theirs[h, z, rows, :]
-                top = jnp.max(jnp.abs(value), axis=0, keepdims=True)
-                power = jnp.floor(jnp.log2(jnp.maximum(top, 1e-30))) + 1.0
-                whole = jnp.clip(jnp.round(value * jnp.exp2(WHOLE - power)), -32767.0, 32767.0)
-                out[chunk, z * half:(z + 1) * half, :] = whole.astype(jnp.int32).astype(jnp.int16)
+                t = h * owners + z
+                start = t * SIDE + b * half
+                value = ours[h, z, b * half:(b + 1) * half, :] + wide(theirs[start:start + half, :]) * scales[t:t + 1, :]
+                whole, power = to_whole(value)
+                out[chunk, z * half:(z + 1) * half, :] = whole
                 powers[z:z + 1, :] = power
-            out[chunk, owners * half:, :] = powers[...].astype(jnp.int32).astype(jnp.int16)
-
-
-def from_whole(sent, out, scales):
+            out[chunk, owners * half:, :] = powers[...].astype(jnp.int32).astype(s16)
+
+
+def add_fours(sent, out, scales):
     chunks = sent.shape[0]
-    owners, half = out.shape[:2]
+    owners = out.shape[0]
+    half = SIDE // 2
     for k in range(chunks):
-        scales[k] = jnp.exp2(sent[k, owners * half:, :].astype(jnp.int32).astype(f32) - WHOLE)
+        scales[k] = scale_of(sent[k, owners * half:, :])
     for z in range(owners):
         value = jnp.zeros((half, SIDE), f32)
         for k in range(chunks):
-            value += sent[k, z * half:(z + 1) * half, :].astype(jnp.int32).astype(f32) * scales[k, z:z + 1, :]
-        root = 0.25 * jnp.sqrt(jnp.abs(value))
-        out[z] = jnp.where(value < 0, -root, root)
-
-
-def stretch(sent):
-    root = sent.astype(f32)
-    return 16.0 * root * jnp.abs(root)
+            value += wide(sent[k, z * half:(z + 1) * half, :]) * scales[k, z:z + 1, :]
+        whole, power = to_whole(value)
+        out[z, :half, :] = whole
+        out[z, half:, :] = jnp.broadcast_to(power, (MARK, SIDE)).astype(jnp.int32).astype(s16)
+
+
+def add_ring(sent, out):
+    owners = sent.shape[0]
+    half = SIDE // 2
+    for b in range(2):
+        value = jnp.zeros((half, SIDE), f32)
+        for z in range(b, owners, 2):
+            value += wide(sent[z, :half, :]) * scale_of(sent[z, half:, :])[:1, :]
+        out[b * half:(b + 1) * half, :] = value
 
 
 def body(tokens, cotangent, gate_tiles, up_tiles, gate_where, up_where, down_where, down_global, down_moment):
@@ -177,37 +213,37 @@
     )(cells, (core * each)[None], tokens, mine)
     hidden_t, away = call(
         functools.partial(second_matrix, col_blocks, row_blocks),
-        (jax.ShapeDtypeStruct((col_blocks * SIDE, count), bf16), sums),
+        (jax.ShapeDtypeStruct((col_blocks * SIDE, count), bf16), jax.ShapeDtypeStruct(((SIDE + 1) * 2 * owners, SIDE), s16)),
         [smem] * 4 + [far] + [vmem] * 3,
-        [pltpu.VMEM(blocks.shape, f32), staged, copies],
+        [pltpu.VMEM(blocks.shape, f32), staged, copies, pltpu.VMEM((2 * owners, SIDE), f32)],
         product * 3 // 2,
         "second_matrix",
     )(cells, ((1 - core) * each)[None], (1 - core)[None], down, theirs, tokens, first, cotangent)
 
     arrived = lax.ppermute(away, "island", other_core)
     stay = call(
-        functools.partial(token_sums, row_blocks), sums, [smem, smem, vmem, vmem], [], 10**11, "token_sums"
+        functools.partial(keep_sums, row_blocks), sums, [smem, smem, vmem, vmem], [], 10**11, "keep_sums"
     )(core[None], down, hidden_t, cotangent)
     half = SIDE // 2
     leaving = call(
-        to_whole,
-        jax.ShapeDtypeStruct((4, (half + 1) * owners, SIDE), jnp.int16),
+        add_cores,
+        jax.ShapeDtypeStruct((4, (half + 1) * owners, SIDE), s16),
         [vmem, vmem],
-        [pltpu.VMEM((owners, SIDE), f32)],
+        [pltpu.VMEM((2 * owners, SIDE), f32), pltpu.VMEM((owners, SIDE), f32)],
         product // 4,
-        "to_whole",
+        "add_cores",
     )(stay, arrived)
     crossed = lax.all_to_all(leaving, ("island", "fsdp"), 0, 0, tiled=True, axis_index_groups=fours)
-    roots = call(
-        from_whole,
-        jax.ShapeDtypeStruct((owners, half, SIDE), f32),
+    halves = call(
+        add_fours,
+        jax.ShapeDtypeStruct((owners, half + MARK, SIDE), s16),
         [vmem],
         [pltpu.VMEM((4, owners, SIDE), f32)],
         product // 4,
-        "from_whole",
+        "add_fours",
     )(crossed)
-    parts = lax.all_to_all(roots.astype(f16), "fsdp", 0, 0, tiled=True)
-    tile = jnp.sum(stretch(parts).reshape(owners // 2, 2, half, SIDE), axis=0).reshape(SIDE, SIDE)
+    parts = lax.all_to_all(halves, "fsdp", 0, 0, tiled=True)
+    tile = call(add_ring, jax.ShapeDtypeStruct((SIDE, SIDE), f32), [vmem], [], product // 4, "add_ring")(parts)
     total = lax.all_gather(tile, "island", axis=0)
 
     master = down_global[:, 0]

time: 133 us -> 134 us (level)
  blocking collectives: 101 us -> 103 us
  waiting for transfers between devices: 2.83 us -> 1.33 us
    ppermute x1, waiting for transfers between devices: 2.82 us -> 1.33 us  [body(): arrived = lax.ppermute(away, 'island', other_core)]
where the time goes in v7:
time: 134 us
  blocking collectives  103 us (77%)
  Pallas kernels  11.7 us (9%)
  starting transfers between devices  10.9 us (8%)
  other arithmetic  5.87 us (4%)
    all_gather x1, blocking collectives, body(): gathered = lax.all_gather(payload, 'fsdp', axis=0)  51.7 us
    all_to_all x1, blocking collectives, body(): lax.all_to_all(leaving, ('island', 'fsdp'), 0, 0, tiled=True, axis_index_...  19.3 us
    all_to_all x1, blocking collectives, body(): parts = lax.all_to_all(halves, 'fsdp', 0, 0, tiled=True)  17.3 us
    all_gather x1, blocking collectives, body(): total = lax.all_gather(tile, 'island', axis=0)  15.2 us
    ppermute x1, starting transfers between devices, body(): theirs = lax.ppermute(mine, 'island', other_core)  9 us
    pallas_call x1, Pallas kernels, body(): call(functools.partial(second_matrix, col_blocks, row_blocks), (jax.Shape...  5.48 us
    pallas_call x1, Pallas kernels, body(): call(first_matrix, blocks, [smem, smem, vmem, far], [staged, copies], pro...  3.72 us
  transfers between devices with their start and end apart: 2, of which 1 were waited for; matrix products, arithmetic and copies ran while one was open for 1% of the time, Pallas kernels for 4%

profile of v7, /device:TPU:1, one launch (start us, length us, event | category | flops | bytes accessed | tf_op | source)
XLA Modules:
  0.0 134.1 jit_solution(13064360039220812048)
XLA Ops:
  0.6 0.8 and_select_fusion.1
  1.4 0.1 fusion.4
  1.5 1.0 multiply_convert_fusion.1
  2.5 0.1 pad_maximum_fusion
  2.6 51.7 %all-gather.2 = f16[16,528,128]{2,1,0:T(8,128)(2,1)S(1)} all-gather(f16[1,528,128]{2,1,0:T(8,128)(2,1)S(1)} %pad_maximum_fusion), channel_id=1, replica_groups=mesh['island'=4,'fsdp'=16,'tensor'=16] {'fsdp'}, dimensions={0}, use_global_device_ids=true | all-gather | bytes 2297856 | tf_op jit(solution)/shard_map/all_gather | solution.py:190
  54.3 1.8 %multiply_convert_fusion.sent = bf16[16,528,128]{2,1,0:T(8,128)(2,1)} fusion(f16[16,528,128]{2,1,0:T(8,128)(2,1)S(1)} %all-gather.2), kind=kLoop, calls=%fused_computation | loop fusion | flops 3244032 | bytes 4325376 | tf_op jit(solution)/shard_map/convert_element_type | solution.py:191
  56.1 9.0 %collective-permute-start = (bf16[16,528,128]{2,1,0:T(8,128)(2,1)}, bf16[16,528,128]{2,1,0:T(8,128)(2,1)}, u32[]{:S(2)}, u32[]{:S(2)}) collective-permute-start(bf16[16,528,128]{2,1,0:T(8,128)(2,1)} %multiply_convert_fusion.sent), channel_id=1, source_target_pairs={{0,256},{256,0},{512,768},{768,512},{1,257},{257,1},{513,769},{769... | collective-permute-start | bytes 6488072 | tf_op jit(solution)/shard_map/ppermute | solution.py:193
  65.1 1.2 convert_reduce_fusion.cells
  66.3 0.0 copy-start.1
  66.3 0.0 copy-start.2
  66.3 3.7 %first_matrix.1.first = f32[18,256,128]{2,1,0:T(8,128)S(1)} custom-call(s32[16,16]{1,0:T(8,128)S(1)} %convert_reduce_fusion.cells, s32[1]{0:T(128)} %bitcast.8.base, bf16[256,4608]{1,0:T(8,128)(2,1)S(1)} %copy-done, bf16[16,528,128]{2,1,0:T(8,128)(2,1)} %multiply_convert_fusion.sent), custom_call_target="tpu_custom_call" | custom-call | flops 536870912 | bytes 8 | tf_op jit(solution)/shard_map/first_matrix/pallas_call | solution.py:206
  70.1 0.0 collective-permute-done.sent
  70.1 0.0 copy-done.1
  70.1 5.5 %second_matrix.1 = (bf16[2304,256]{1,0:T(8,128)(2,1)S(1)}, s16[4128,128]{1,0:T(8,128)(2,1)S(1)}) custom-call(s32[16,16]{1,0:T(8,128)S(1)} %convert_reduce_fusion.cells, s32[1]{0:T(128)} %bitcast.6.base, s32[1]{0:T(128)} %bitcast.7.side, s32[64]{0:T(128)S(1)} %bitcast.40, bf16[16,528,128]{2,1,0:T(8,128)(2,1)} %collective-permute-done.sent, ...), custom_call_target="tpu_custom_call" | custom-call | flops 805306368 | bytes 8 | tf_op jit(solution)/shard_map/second_matrix/pallas_call | solution.py:214
  75.6 1.9 %collective-permute-start.1 = (s16[4128,128]{1,0:T(8,128)(2,1)S(1)}, s16[4128,128]{1,0:T(8,128)(2,1)S(1)}, u32[]{:S(2)}, u32[]{:S(2)}) collective-permute-start(s16[4128,128]{1,0:T(8,128)(2,1)S(1)} %get-tuple-element.5), channel_id=1, source_target_pairs={{0,256},{256,0},{512,768},{768,512},{1,257},{257,1},{513,769},{769... | collective-permute-start | bytes 3170312 | tf_op jit(solution)/shard_map/ppermute | solution.py:223
  77.5 1.3 keep_sums.1.ours
  78.8 1.3 collective-permute-done.1.theirs
  80.1 0.8 add_cores.1
  80.9 19.3 %all_to_all.10.sent = s16[4,1040,128]{2,1,0:T(8,128)(2,1)S(1)} all-to-all(s16[4,1040,128]{2,1,0:T(8,128)(2,1)S(1)} %add_cores.1), channel_id=1, replica_groups={{0,16,512,528},{32,48,544,560},{64,80,576,592},{96,112,608,624},{128,14..., dimensions={0} | all-to-all | bytes 2129920 | tf_op jit(solution)/shard_map/all_to_all | solution.py:236
  100.2 0.4 add_fours.1
  100.6 17.3 %all_to_all.11.sent = s16[16,80,128]{2,1,0:T(8,128)(2,1)S(1)} all-to-all(s16[16,80,128]{2,1,0:T(8,128)(2,1)S(1)} %add_fours.1), channel_id=1, replica_groups=mesh['island'=4,'fsdp'=16,'tensor'=16] {'fsdp'}, dimensions={0} | all-to-all | bytes 655360 | tf_op jit(solution)/shard_map/all_to_all | solution.py:245
  117.9 0.1 add_ring.1
  118.0 15.2 %all-gather = f32[512,128]{1,0:T(8,128)S(1)} all-gather(f32[128,128]{1,0:T(8,128)S(1)} %add_ring.1), channel_id=2, replica_groups=mesh['island'=4,'fsdp'=16,'tensor'=16] {'island'}, dimensions={0}, use_global_device_ids=true | all-gather | bytes 327680 | tf_op jit(solution)/shard_map/all_gather | solution.py:247
  133.2 0.9 fusion.3
  (9 shorter events, 0.0 us)
Async XLA Ops:
  54.3 12.0 %copy-start = (bf16[256,4608]{1,0:T(8,128)(2,1)S(1)}, bf16[256,4608]{1,0:T(8,128)(2,1)}, u32[]{:S(2)}) copy-start(bf16[256,4608]{1,0:T(8,128)(2,1)} %tok.3) | copy-start | bytes 7077892
  56.1 14.0 %collective-permute-start = (bf16[16,528,128]{2,1,0:T(8,128)(2,1)}, bf16[16,528,128]{2,1,0:T(8,128)(2,1)}, u32[]{:S(2)}, u32[]{:S(2)}) collective-permute-start(bf16[16,528,128]{2,1,0:T(8,128)(2,1)} %multiply_convert_fusion.sent), channel_id=1, source_target_pairs={{0,256},{256,0},{512,768},{768,512},{1,257},{257,1},{513,769},{769... | collective-permute-start | bytes 6488072 | tf_op jit(solution)/shard_map/ppermute | solution.py:193
  66.3 3.8 %copy-start.1 = (bf16[256,4608]{1,0:T(8,128)(2,1)S(1)}, bf16[256,4608]{1,0:T(8,128)(2,1)}, u32[]{:S(2)}) copy-start(bf16[256,4608]{1,0:T(8,128)(2,1)} %cot.3) | copy-start | bytes 7077892
  66.3 3.8 %copy-start.2 = (s32[64,1]{0,1:T(1,128)S(1)}, s32[64,1]{0,1:T(1,128)}, u32[]{:S(2)}) copy-start(s32[64,1]{0,1:T(1,128)} %param.15) | copy-start | bytes 772
  75.6 4.6 %collective-permute-start.1 = (s16[4128,128]{1,0:T(8,128)(2,1)S(1)}, s16[4128,128]{1,0:T(8,128)(2,1)S(1)}, u32[]{:S(2)}, u32[]{:S(2)}) collective-permute-start(s16[4128,128]{1,0:T(8,128)(2,1)S(1)} %get-tuple-element.5), channel_id=1, source_target_pairs={{0,256},{256,0},{512,768},{768,512},{1,257},{257,1},{513,769},{769... | collective-permute-start | bytes 3170312 | tf_op jit(solution)/shard_map/ppermute | solution.py:223
  100.2 33.0 %copy-start.3 = (f32[4,1,128,128]{3,2,1,0:T(8,128)S(1)}, f32[4,1,128,128]{3,2,1,0:T(8,128)}, u32[]{:S(2)}) copy-start(f32[4,1,128,128]{3,2,1,0:T(8,128)} %param.17) | copy-start | bytes 786436
  100.2 33.0 %copy-start.4 = (f32[4,1,128,128]{3,2,1,0:T(8,128)S(1)}, f32[4,1,128,128]{3,2,1,0:T(8,128)}, u32[]{:S(2)}) copy-start(f32[4,1,128,128]{3,2,1,0:T(8,128)} %param.16) | copy-start | bytes 786436

commit v8 on v7

--- a/solution.py
+++ b/solution.py
@@ -11,7 +11,6 @@
 SIDE = 128
 TILE_SCALE = 2.0**17
 WHOLE = 15.0
-MARK = 16
 
 inner_rate = 0.5
 decay_rate = 0.1
@@ -145,27 +144,20 @@
 
 def add_fours(sent, out, scales):
     chunks = sent.shape[0]
-    owners = out.shape[0]
-    half = SIDE // 2
+    owners, half = out.shape[:2]
     for k in range(chunks):
         scales[k] = scale_of(sent[k, owners * half:, :])
     for z in range(owners):
         value = jnp.zeros((half, SIDE), f32)
         for k in range(chunks):
             value += wide(sent[k, z * half:(z + 1) * half, :]) * scales[k, z:z + 1, :]
-        whole, power = to_whole(value)
-        out[z, :half, :] = whole
-        out[z, half:, :] = jnp.broadcast_to(power, (MARK, SIDE)).astype(jnp.int32).astype(s16)
-
-
-def add_ring(sent, out):
-    owners = sent.shape[0]
-    half = SIDE // 2
-    for b in range(2):
-        value = jnp.zeros((half, SIDE), f32)
-        for z in range(b, owners, 2):
-            value += wide(sent[z, :half, :]) * scale_of(sent[z, half:, :])[:1, :]
-        out[b * half:(b + 1) * half, :] = value
+        root = 0.25 * jnp.sqrt(jnp.abs(value))
+        out[z] = jnp.where(value < 0, -root, root)
+
+
+def stretch(sent):
+    root = sent.astype(f32)
+    return 16.0 * root * jnp.abs(root)
 
 
 def body(tokens, cotangent, gate_tiles, up_tiles, gate_where, up_where, down_where, down_global, down_moment):
@@ -234,16 +226,16 @@
         "add_cores",
     )(stay, arrived)
     crossed = lax.all_to_all(leaving, ("island", "fsdp"), 0, 0, tiled=True, axis_index_groups=fours)
-    halves = call(
+    roots = call(
         add_fours,
-        jax.ShapeDtypeStruct((owners, half + MARK, SIDE), s16),
+        jax.ShapeDtypeStruct((owners, half, SIDE), f32),
         [vmem],
         [pltpu.VMEM((4, owners, SIDE), f32)],
         product // 4,
         "add_fours",
     )(crossed)
-    parts = lax.all_to_all(halves, "fsdp", 0, 0, tiled=True)
-    tile = call(add_ring, jax.ShapeDtypeStruct((SIDE, SIDE), f32), [vmem], [], product // 4, "add_ring")(parts)
+    parts = lax.all_to_all(roots.astype(f16), "fsdp", 0, 0, tiled=True)
+    tile = jnp.sum(stretch(parts).reshape(owners // 2, 2, half, SIDE), axis=0).reshape(SIDE, SIDE)
     total = lax.all_gather(tile, "island", axis=0)
 
     master = down_global[:, 0]

time: 134 us -> 132 us (0.985)
  blocking collectives: 103 us -> 101 us
where the time goes in v8:
time: 132 us
  blocking collectives  101 us (77%)
  Pallas kernels  11.7 us (9%)
  starting transfers between devices  10.9 us (8%)
  other arithmetic  6.02 us (5%)
  waiting for transfers between devices  1.35 us (1%)
    all_gather x1, blocking collectives, body(): gathered = lax.all_gather(payload, 'fsdp', axis=0)  51.7 us
    all_to_all x1, blocking collectives, body(): lax.all_to_all(leaving, ('island', 'fsdp'), 0, 0, tiled=True, axis_index_...  19.3 us
    all_to_all x1, blocking collectives, body(): parts = lax.all_to_all(roots.astype(f16), 'fsdp', 0, 0, tiled=True)  16.2 us
    all_gather x1, blocking collectives, body(): total = lax.all_gather(tile, 'island', axis=0)  13.9 us
    ppermute x1, starting transfers between devices, body(): theirs = lax.ppermute(mine, 'island', other_core)  9 us
    pallas_call x1, Pallas kernels, body(): call(functools.partial(second_matrix, col_blocks, row_blocks), (jax.Shape...  5.5 us
    pallas_call x1, Pallas kernels, body(): call(first_matrix, blocks, [smem, smem, vmem, far], [staged, copies], pro...  3.73 us
  transfers between devices with their start and end apart: 2, of which 1 were waited for; matrix products, arithmetic and copies ran while one was open for 1% of the time, Pallas kernels for 4%

profile of v8, /device:TPU:1, one launch (start us, length us, event | category | flops | bytes accessed | tf_op | source)
XLA Modules:
  0.0 131.8 jit_solution(10551478563863729924)
XLA Ops:
  0.6 0.8 and_select_fusion.1
  1.4 0.1 fusion.5
  1.5 1.0 multiply_convert_fusion.1
  2.5 0.1 pad_maximum_fusion
  2.6 51.7 %all-gather.1 = f16[16,528,128]{2,1,0:T(8,128)(2,1)S(1)} all-gather(f16[1,528,128]{2,1,0:T(8,128)(2,1)S(1)} %pad_maximum_fusion), channel_id=1, replica_groups=mesh['island'=4,'fsdp'=16,'tensor'=16] {'fsdp'}, dimensions={0}, use_global_device_ids=true | all-gather | bytes 2297856 | tf_op jit(solution)/shard_map/all_gather | solution.py:182
  54.3 1.9 %multiply_convert_fusion.sent = bf16[16,528,128]{2,1,0:T(8,128)(2,1)} fusion(f16[16,528,128]{2,1,0:T(8,128)(2,1)S(1)} %all-gather.1), kind=kLoop, calls=%fused_computation | loop fusion | flops 3244032 | bytes 4325376 | tf_op jit(solution)/shard_map/convert_element_type | solution.py:183
  56.1 9.0 %collective-permute-start = (bf16[16,528,128]{2,1,0:T(8,128)(2,1)}, bf16[16,528,128]{2,1,0:T(8,128)(2,1)}, u32[]{:S(2)}, u32[]{:S(2)}) collective-permute-start(bf16[16,528,128]{2,1,0:T(8,128)(2,1)} %multiply_convert_fusion.sent), channel_id=1, source_target_pairs={{0,256},{256,0},{512,768},{768,512},{1,257},{257,1},{513,769},{769... | collective-permute-start | bytes 6488072 | tf_op jit(solution)/shard_map/ppermute | solution.py:185
  65.1 1.2 convert_reduce_fusion.cells
  66.3 0.0 copy-start.1
  66.3 0.0 copy-start.2
  66.3 3.7 %first_matrix.1.first = f32[18,256,128]{2,1,0:T(8,128)S(1)} custom-call(s32[16,16]{1,0:T(8,128)S(1)} %convert_reduce_fusion.cells, s32[1]{0:T(128)} %bitcast.8.base, bf16[256,4608]{1,0:T(8,128)(2,1)S(1)} %copy-done, bf16[16,528,128]{2,1,0:T(8,128)(2,1)} %multiply_convert_fusion.sent), custom_call_target="tpu_custom_call" | custom-call | flops 536870912 | bytes 8 | tf_op jit(solution)/shard_map/first_matrix/pallas_call | solution.py:198
  70.1 0.0 collective-permute-done.sent
  70.1 5.5 %second_matrix.1 = (bf16[2304,256]{1,0:T(8,128)(2,1)S(1)}, s16[4128,128]{1,0:T(8,128)(2,1)S(1)}) custom-call(s32[16,16]{1,0:T(8,128)S(1)} %convert_reduce_fusion.cells, s32[1]{0:T(128)} %bitcast.6.base, s32[1]{0:T(128)} %bitcast.7.side, s32[64]{0:T(128)S(1)} %bitcast.49, bf16[16,528,128]{2,1,0:T(8,128)(2,1)} %collective-permute-done.sent, ...), custom_call_target="tpu_custom_call" | custom-call | flops 805306368 | bytes 8 | tf_op jit(solution)/shard_map/second_matrix/pallas_call | solution.py:206
  75.6 1.9 %collective-permute-start.1 = (s16[4128,128]{1,0:T(8,128)(2,1)S(1)}, s16[4128,128]{1,0:T(8,128)(2,1)S(1)}, u32[]{:S(2)}, u32[]{:S(2)}) collective-permute-start(s16[4128,128]{1,0:T(8,128)(2,1)S(1)} %get-tuple-element.5), channel_id=1, source_target_pairs={{0,256},{256,0},{512,768},{768,512},{1,257},{257,1},{513,769},{769... | collective-permute-start | bytes 3170312 | tf_op jit(solution)/shard_map/ppermute | solution.py:215
  77.6 1.3 keep_sums.1.ours
  78.8 1.3 %collective-permute-done.1.theirs = s16[4128,128]{1,0:T(8,128)(2,1)S(1)} collective-permute-done((s16[4128,128]{1,0:T(8,128)(2,1)S(1)}, s16[4128,128]{1,0:T(8,128)(2,1)S(1)}, u32[]{:S(2)}, u32[]{:S(2)}) %collective-permute-start.1) | collective-permute-done | bytes 1056800 | tf_op jit(solution)/shard_map/ppermute | solution.py:215
  80.2 0.8 add_cores.1
  81.0 19.3 %all_to_all.10.sent = s16[4,1040,128]{2,1,0:T(8,128)(2,1)S(1)} all-to-all(s16[4,1040,128]{2,1,0:T(8,128)(2,1)S(1)} %add_cores.1), channel_id=1, replica_groups={{0,16,512,528},{32,48,544,560},{64,80,576,592},{96,112,608,624},{128,14..., dimensions={0} | all-to-all | bytes 2129920 | tf_op jit(solution)/shard_map/all_to_all | solution.py:228
  100.3 0.5 add_fours.1
  100.8 16.2 %all_to_all.11 = f16[16,64,128]{2,1,0:T(8,128)(2,1)S(1)} all-to-all(f16[16,64,128]{2,1,0:T(8,128)(2,1)S(1)} %convert_element_type.54), channel_id=1, replica_groups=mesh['island'=4,'fsdp'=16,'tensor'=16] {'fsdp'}, dimensions={0} | all-to-all | bytes 524288 | tf_op jit(solution)/shard_map/all_to_all | solution.py:237
  116.9 0.1 fusion
  117.1 13.9 %all_gather.8 = f32[4,128,128]{2,1,0:T(8,128)S(1)} all-gather(f32[1,128,128]{2,1,0:T(8,128)S(1)} %bitcast.53), channel_id=1, replica_groups=mesh['island'=4,'fsdp'=16,'tensor'=16] {'island'}, dimensions={0}, use_global_device_ids=true | all-gather | bytes 327680 | tf_op jit(solution)/shard_map/all_gather | solution.py:239
  130.9 0.0 copy-done.4
  130.9 0.9 fusion.4
  (10 shorter events, 0.1 us)
Async XLA Ops:
  54.3 12.1 %copy-start = (bf16[256,4608]{1,0:T(8,128)(2,1)S(1)}, bf16[256,4608]{1,0:T(8,128)(2,1)}, u32[]{:S(2)}) copy-start(bf16[256,4608]{1,0:T(8,128)(2,1)} %tok.3) | copy-start | bytes 7077892
  56.1 14.0 %collective-permute-start = (bf16[16,528,128]{2,1,0:T(8,128)(2,1)}, bf16[16,528,128]{2,1,0:T(8,128)(2,1)}, u32[]{:S(2)}, u32[]{:S(2)}) collective-permute-start(bf16[16,528,128]{2,1,0:T(8,128)(2,1)} %multiply_convert_fusion.sent), channel_id=1, source_target_pairs={{0,256},{256,0},{512,768},{768,512},{1,257},{257,1},{513,769},{769... | collective-permute-start | bytes 6488072 | tf_op jit(solution)/shard_map/ppermute | solution.py:185
  66.3 3.8 %copy-start.1 = (bf16[256,4608]{1,0:T(8,128)(2,1)S(1)}, bf16[256,4608]{1,0:T(8,128)(2,1)}, u32[]{:S(2)}) copy-start(bf16[256,4608]{1,0:T(8,128)(2,1)} %cot.3) | copy-start | bytes 7077892
  66.3 3.8 %copy-start.2 = (s32[64,1]{0,1:T(1,128)S(1)}, s32[64,1]{0,1:T(1,128)}, u32[]{:S(2)}) copy-start(s32[64,1]{0,1:T(1,128)} %param.15) | copy-start | bytes 772
  75.6 4.6 %collective-permute-start.1 = (s16[4128,128]{1,0:T(8,128)(2,1)S(1)}, s16[4128,128]{1,0:T(8,128)(2,1)S(1)}, u32[]{:S(2)}, u32[]{:S(2)}) collective-permute-start(s16[4128,128]{1,0:T(8,128)(2,1)S(1)} %get-tuple-element.5), channel_id=1, source_target_pairs={{0,256},{256,0},{512,768},{768,512},{1,257},{257,1},{513,769},{769... | collective-permute-start | bytes 3170312 | tf_op jit(solution)/shard_map/ppermute | solution.py:215
  100.2 30.7 %copy-start.3 = (f32[4,1,128,128]{3,2,1,0:T(8,128)S(1)}, f32[4,1,128,128]{3,2,1,0:T(8,128)}, u32[]{:S(2)}) copy-start(f32[4,1,128,128]{3,2,1,0:T(8,128)} %param.16) | copy-start | bytes 786436
  100.2 30.7 %copy-start.4 = (f32[4,1,128,128]{3,2,1,0:T(8,128)S(1)}, f32[4,1,128,128]{3,2,1,0:T(8,128)}, u32[]{:S(2)}) copy-start(f32[4,1,128,128]{3,2,1,0:T(8,128)} %param.17) | copy-start | bytes 786436

commit v9 on v8

--- a/solution.py
+++ b/solution.py
@@ -30,7 +30,7 @@
 def add_products(cells, base, tok, sent, tiles, sems, acc):
     owners = cells.shape[0]
     each = cells.shape[1] // 4
-    together = 4
+    together = 2
     groups = owners // together
 
     def fetch(group):
@@ -88,7 +88,7 @@
 ):
     add_products(cells, base[0], tok, sent, tiles, sems, acc)
     first_is_gate = base[0] != 0
-    together = 6
+    together = 9
 
     def activate(group, carry):
         for near in range(together):
@@ -194,7 +194,7 @@
     product = 2 * kept * count * SIDE * SIDE
 
     staged = pltpu.VMEM((owners, each * SIDE, SIDE), bf16)
-    copies = pltpu.SemaphoreType.DMA((owners // 4,))
+    copies = pltpu.SemaphoreType.DMA((owners // 2,))
     first = call(
         first_matrix,
         blocks,

time: 132 us -> 133 us (level)
  no operation moved by 1% of the time
where the time goes in v9:
time: 133 us
  blocking collectives  101 us (76%)
  Pallas kernels  12.7 us (10%)
  starting transfers between devices  10.9 us (8%)
  other arithmetic  6.02 us (5%)
  waiting for transfers between devices  1.34 us (1%)
    all_gather x1, blocking collectives, body(): gathered = lax.all_gather(payload, 'fsdp', axis=0)  51.7 us
    all_to_all x1, blocking collectives, body(): lax.all_to_all(leaving, ('island', 'fsdp'), 0, 0, tiled=True, axis_index_...  19.3 us
    all_to_all x1, blocking collectives, body(): parts = lax.all_to_all(roots.astype(f16), 'fsdp', 0, 0, tiled=True)  16.2 us
    all_gather x1, blocking collectives, body(): total = lax.all_gather(tile, 'island', axis=0)  13.9 us
    ppermute x1, starting transfers between devices, body(): theirs = lax.ppermute(mine, 'island', other_core)  9 us
    pallas_call x1, Pallas kernels, body(): call(functools.partial(second_matrix, col_blocks, row_blocks), (jax.Shape...  5.97 us
    pallas_call x1, Pallas kernels, body(): call(first_matrix, blocks, [smem, smem, vmem, far], [staged, copies], pro...  4.23 us
  transfers between devices with their start and end apart: 2, of which 1 were waited for; matrix products, arithmetic and copies ran while one was open for 1% of the time, Pallas kernels for 4%

profile of v9, /device:TPU:1, one launch (start us, length us, event | category | flops | bytes accessed | tf_op | source)
XLA Modules:
  0.0 132.8 jit_solution(15374398656996440041)
XLA Ops:
  0.6 0.8 and_select_fusion.1
  1.4 0.1 fusion.5
  1.5 1.0 multiply_convert_fusion.1
  2.5 0.1 pad_maximum_fusion
  2.6 51.7 %all-gather.1 = f16[16,528,128]{2,1,0:T(8,128)(2,1)S(1)} all-gather(f16[1,528,128]{2,1,0:T(8,128)(2,1)S(1)} %pad_maximum_fusion), channel_id=1, replica_groups=mesh['island'=4,'fsdp'=16,'tensor'=16] {'fsdp'}, dimensions={0}, use_global_device_ids=true | all-gather | bytes 2297856 | tf_op jit(solution)/shard_map/all_gather | solution.py:182
  54.3 1.9 %multiply_convert_fusion.sent = bf16[16,528,128]{2,1,0:T(8,128)(2,1)} fusion(f16[16,528,128]{2,1,0:T(8,128)(2,1)S(1)} %all-gather.1), kind=kLoop, calls=%fused_computation | loop fusion | flops 3244032 | bytes 4325376 | tf_op jit(solution)/shard_map/convert_element_type | solution.py:183
  56.1 9.0 %collective-permute-start = (bf16[16,528,128]{2,1,0:T(8,128)(2,1)}, bf16[16,528,128]{2,1,0:T(8,128)(2,1)}, u32[]{:S(2)}, u32[]{:S(2)}) collective-permute-start(bf16[16,528,128]{2,1,0:T(8,128)(2,1)} %multiply_convert_fusion.sent), channel_id=1, source_target_pairs={{0,256},{256,0},{512,768},{768,512},{1,257},{257,1},{513,769},{769... | collective-permute-start | bytes 6488072 | tf_op jit(solution)/shard_map/ppermute | solution.py:185
  65.1 1.2 convert_reduce_fusion.cells
  66.3 0.0 copy-start.1
  66.3 0.0 copy-start.2
  66.3 4.2 %first_matrix.1.first = f32[18,256,128]{2,1,0:T(8,128)S(1)} custom-call(s32[16,16]{1,0:T(8,128)S(1)} %convert_reduce_fusion.cells, s32[1]{0:T(128)} %bitcast.8.base, bf16[256,4608]{1,0:T(8,128)(2,1)S(1)} %copy-done, bf16[16,528,128]{2,1,0:T(8,128)(2,1)} %multiply_convert_fusion.sent), custom_call_target="tpu_custom_call" | custom-call | flops 536870912 | bytes 8 | tf_op jit(solution)/shard_map/first_matrix/pallas_call | solution.py:198
  70.6 0.0 collective-permute-done.sent
  70.6 6.0 %second_matrix.1 = (bf16[2304,256]{1,0:T(8,128)(2,1)S(1)}, s16[4128,128]{1,0:T(8,128)(2,1)S(1)}) custom-call(s32[16,16]{1,0:T(8,128)S(1)} %convert_reduce_fusion.cells, s32[1]{0:T(128)} %bitcast.6.base, s32[1]{0:T(128)} %bitcast.7.side, s32[64]{0:T(128)S(1)} %bitcast.49, bf16[16,528,128]{2,1,0:T(8,128)(2,1)} %collective-permute-done.sent, ...), custom_call_target="tpu_custom_call" | custom-call | flops 805306368 | bytes 8 | tf_op jit(solution)/shard_map/second_matrix/pallas_call | solution.py:206
  76.6 1.9 %collective-permute-start.1 = (s16[4128,128]{1,0:T(8,128)(2,1)S(1)}, s16[4128,128]{1,0:T(8,128)(2,1)S(1)}, u32[]{:S(2)}, u32[]{:S(2)}) collective-permute-start(s16[4128,128]{1,0:T(8,128)(2,1)S(1)} %get-tuple-element.5), channel_id=1, source_target_pairs={{0,256},{256,0},{512,768},{768,512},{1,257},{257,1},{513,769},{769... | collective-permute-start | bytes 3170312 | tf_op jit(solution)/shard_map/ppermute | solution.py:215
  78.5 1.3 keep_sums.1.ours
  79.8 1.3 %collective-permute-done.1.theirs = s16[4128,128]{1,0:T(8,128)(2,1)S(1)} collective-permute-done((s16[4128,128]{1,0:T(8,128)(2,1)S(1)}, s16[4128,128]{1,0:T(8,128)(2,1)S(1)}, u32[]{:S(2)}, u32[]{:S(2)}) %collective-permute-start.1) | collective-permute-done | bytes 1056800 | tf_op jit(solution)/shard_map/ppermute | solution.py:215
  81.2 0.8 add_cores.1
  81.9 19.3 %all_to_all.10.sent = s16[4,1040,128]{2,1,0:T(8,128)(2,1)S(1)} all-to-all(s16[4,1040,128]{2,1,0:T(8,128)(2,1)S(1)} %add_cores.1), channel_id=1, replica_groups={{0,16,512,528},{32,48,544,560},{64,80,576,592},{96,112,608,624},{128,14..., dimensions={0} | all-to-all | bytes 2129920 | tf_op jit(solution)/shard_map/all_to_all | solution.py:228
  101.2 0.5 add_fours.1
  101.7 16.2 %all_to_all.11 = f16[16,64,128]{2,1,0:T(8,128)(2,1)S(1)} all-to-all(f16[16,64,128]{2,1,0:T(8,128)(2,1)S(1)} %convert_element_type.54), channel_id=1, replica_groups=mesh['island'=4,'fsdp'=16,'tensor'=16] {'fsdp'}, dimensions={0} | all-to-all | bytes 524288 | tf_op jit(solution)/shard_map/all_to_all | solution.py:237
  117.9 0.1 fusion
  118.0 13.9 %all_gather.8 = f32[4,128,128]{2,1,0:T(8,128)S(1)} all-gather(f32[1,128,128]{2,1,0:T(8,128)S(1)} %bitcast.53), channel_id=1, replica_groups=mesh['island'=4,'fsdp'=16,'tensor'=16] {'island'}, dimensions={0}, use_global_device_ids=true | all-gather | bytes 327680 | tf_op jit(solution)/shard_map/all_gather | solution.py:239
  131.9 0.0 copy-done.4
  131.9 0.9 fusion.4
  (10 shorter events, 0.1 us)
Async XLA Ops:
  54.3 12.1 %copy-start = (bf16[256,4608]{1,0:T(8,128)(2,1)S(1)}, bf16[256,4608]{1,0:T(8,128)(2,1)}, u32[]{:S(2)}) copy-start(bf16[256,4608]{1,0:T(8,128)(2,1)} %tok.3) | copy-start | bytes 7077892
  56.1 14.5 %collective-permute-start = (bf16[16,528,128]{2,1,0:T(8,128)(2,1)}, bf16[16,528,128]{2,1,0:T(8,128)(2,1)}, u32[]{:S(2)}, u32[]{:S(2)}) collective-permute-start(bf16[16,528,128]{2,1,0:T(8,128)(2,1)} %multiply_convert_fusion.sent), channel_id=1, source_target_pairs={{0,256},{256,0},{512,768},{768,512},{1,257},{257,1},{513,769},{769... | collective-permute-start | bytes 6488072 | tf_op jit(solution)/shard_map/ppermute | solution.py:185
  66.3 4.3 %copy-start.1 = (bf16[256,4608]{1,0:T(8,128)(2,1)S(1)}, bf16[256,4608]{1,0:T(8,128)(2,1)}, u32[]{:S(2)}) copy-start(bf16[256,4608]{1,0:T(8,128)(2,1)} %cot.3) | copy-start | bytes 7077892
  66.3 4.3 %copy-start.2 = (s32[64,1]{0,1:T(1,128)S(1)}, s32[64,1]{0,1:T(1,128)}, u32[]{:S(2)}) copy-start(s32[64,1]{0,1:T(1,128)} %param.15) | copy-start | bytes 772
  76.6 4.6 %collective-permute-start.1 = (s16[4128,128]{1,0:T(8,128)(2,1)S(1)}, s16[4128,128]{1,0:T(8,128)(2,1)S(1)}, u32[]{:S(2)}, u32[]{:S(2)}) collective-permute-start(s16[4128,128]{1,0:T(8,128)(2,1)S(1)} %get-tuple-element.5), channel_id=1, source_target_pairs={{0,256},{256,0},{512,768},{768,512},{1,257},{257,1},{513,769},{769... | collective-permute-start | bytes 3170312 | tf_op jit(solution)/shard_map/ppermute | solution.py:215
  101.2 30.7 %copy-start.3 = (f32[4,1,128,128]{3,2,1,0:T(8,128)S(1)}, f32[4,1,128,128]{3,2,1,0:T(8,128)}, u32[]{:S(2)}) copy-start(f32[4,1,128,128]{3,2,1,0:T(8,128)} %param.16) | copy-start | bytes 786436
  101.2 30.7 %copy-start.4 = (f32[4,1,128,128]{3,2,1,0:T(8,128)S(1)}, f32[4,1,128,128]{3,2,1,0:T(8,128)}, u32[]{:S(2)}) copy-start(f32[4,1,128,128]{3,2,1,0:T(8,128)} %param.17) | copy-start | bytes 786436

commit v10 on v9

--- a/solution.py
+++ b/solution.py
@@ -30,7 +30,7 @@
 def add_products(cells, base, tok, sent, tiles, sems, acc):
     owners = cells.shape[0]
     each = cells.shape[1] // 4
-    together = 2
+    together = 8
     groups = owners // together
 
     def fetch(group):
@@ -194,7 +194,7 @@
     product = 2 * kept * count * SIDE * SIDE
 
     staged = pltpu.VMEM((owners, each * SIDE, SIDE), bf16)
-    copies = pltpu.SemaphoreType.DMA((owners // 2,))
+    copies = pltpu.SemaphoreType.DMA((owners // 8,))
     first = call(
         first_matrix,
         blocks,

time: 133 us -> 132 us (level)
  no operation moved by 1% of the time
where the time goes in v10:
time: 132 us; the launch traced here: 131 us
  blocking collectives  101 us (77%)
  Pallas kernels  11.5 us (9%)
  starting transfers between devices  10.9 us (8%)
  other arithmetic  6.02 us (5%)
  waiting for transfers between devices  1.35 us (1%)
    all_gather x1, blocking collectives, body(): gathered = lax.all_gather(payload, 'fsdp', axis=0)  51.7 us
    all_to_all x1, blocking collectives, body(): lax.all_to_all(leaving, ('island', 'fsdp'), 0, 0, tiled=True, axis_index_...  19.3 us
    all_to_all x1, blocking collectives, body(): parts = lax.all_to_all(roots.astype(f16), 'fsdp', 0, 0, tiled=True)  16.2 us
    all_gather x1, blocking collectives, body(): total = lax.all_gather(tile, 'island', axis=0)  13.9 us
    ppermute x1, starting transfers between devices, body(): theirs = lax.ppermute(mine, 'island', other_core)  9 us
    pallas_call x1, Pallas kernels, body(): call(functools.partial(second_matrix, col_blocks, row_blocks), (jax.Shape...  5.33 us
    pallas_call x1, Pallas kernels, body(): call(first_matrix, blocks, [smem, smem, vmem, far], [staged, copies], pro...  3.6 us
  transfers between devices with their start and end apart: 2, of which 1 were waited for; matrix products, arithmetic and copies ran while one was open for 1% of the time, Pallas kernels for 4%

profile of v10, /device:TPU:1, one launch (start us, length us, event | category | flops | bytes accessed | tf_op | source)
XLA Modules:
  0.0 131.5 jit_solution(15947852847467682815)
XLA Ops:
  0.6 0.8 and_select_fusion.1
  1.4 0.1 fusion.5
  1.5 1.0 multiply_convert_fusion.1
  2.5 0.1 pad_maximum_fusion
  2.6 51.7 %all-gather.1 = f16[16,528,128]{2,1,0:T(8,128)(2,1)S(1)} all-gather(f16[1,528,128]{2,1,0:T(8,128)(2,1)S(1)} %pad_maximum_fusion), channel_id=1, replica_groups=mesh['island'=4,'fsdp'=16,'tensor'=16] {'fsdp'}, dimensions={0}, use_global_device_ids=true | all-gather | bytes 2297856 | tf_op jit(solution)/shard_map/all_gather | solution.py:182
  54.3 1.9 %multiply_convert_fusion.sent = bf16[16,528,128]{2,1,0:T(8,128)(2,1)} fusion(f16[16,528,128]{2,1,0:T(8,128)(2,1)S(1)} %all-gather.1), kind=kLoop, calls=%fused_computation | loop fusion | flops 3244032 | bytes 4325376 | tf_op jit(solution)/shard_map/convert_element_type | solution.py:183
  56.1 9.0 %collective-permute-start = (bf16[16,528,128]{2,1,0:T(8,128)(2,1)}, bf16[16,528,128]{2,1,0:T(8,128)(2,1)}, u32[]{:S(2)}, u32[]{:S(2)}) collective-permute-start(bf16[16,528,128]{2,1,0:T(8,128)(2,1)} %multiply_convert_fusion.sent), channel_id=1, source_target_pairs={{0,256},{256,0},{512,768},{768,512},{1,257},{257,1},{513,769},{769... | collective-permute-start | bytes 6488072 | tf_op jit(solution)/shard_map/ppermute | solution.py:185
  65.1 1.2 convert_reduce_fusion.cells
  66.3 0.0 copy-start.1
  66.3 0.0 copy-start.2
  66.3 3.6 %first_matrix.1.first = f32[18,256,128]{2,1,0:T(8,128)S(1)} custom-call(s32[16,16]{1,0:T(8,128)S(1)} %convert_reduce_fusion.cells, s32[1]{0:T(128)} %bitcast.8.base, bf16[256,4608]{1,0:T(8,128)(2,1)S(1)} %copy-done, bf16[16,528,128]{2,1,0:T(8,128)(2,1)} %multiply_convert_fusion.sent), custom_call_target="tpu_custom_call" | custom-call | flops 536870912 | bytes 8 | tf_op jit(solution)/shard_map/first_matrix/pallas_call | solution.py:198
  70.0 0.0 collective-permute-done.sent
  70.0 5.3 %second_matrix.1 = (bf16[2304,256]{1,0:T(8,128)(2,1)S(1)}, s16[4128,128]{1,0:T(8,128)(2,1)S(1)}) custom-call(s32[16,16]{1,0:T(8,128)S(1)} %convert_reduce_fusion.cells, s32[1]{0:T(128)} %bitcast.6.base, s32[1]{0:T(128)} %bitcast.7.side, s32[64]{0:T(128)S(1)} %bitcast.49, bf16[16,528,128]{2,1,0:T(8,128)(2,1)} %collective-permute-done.sent, ...), custom_call_target="tpu_custom_call" | custom-call | flops 805306368 | bytes 8 | tf_op jit(solution)/shard_map/second_matrix/pallas_call | solution.py:206
  75.3 1.9 %collective-permute-start.1 = (s16[4128,128]{1,0:T(8,128)(2,1)S(1)}, s16[4128,128]{1,0:T(8,128)(2,1)S(1)}, u32[]{:S(2)}, u32[]{:S(2)}) collective-permute-start(s16[4128,128]{1,0:T(8,128)(2,1)S(1)} %get-tuple-element.5), channel_id=1, source_target_pairs={{0,256},{256,0},{512,768},{768,512},{1,257},{257,1},{513,769},{769... | collective-permute-start | bytes 3170312 | tf_op jit(solution)/shard_map/ppermute | solution.py:215
  77.2 1.3 keep_sums.1.ours
  78.5 1.3 %collective-permute-done.1.theirs = s16[4128,128]{1,0:T(8,128)(2,1)S(1)} collective-permute-done((s16[4128,128]{1,0:T(8,128)(2,1)S(1)}, s16[4128,128]{1,0:T(8,128)(2,1)S(1)}, u32[]{:S(2)}, u32[]{:S(2)}) %collective-permute-start.1) | collective-permute-done | bytes 1056800 | tf_op jit(solution)/shard_map/ppermute | solution.py:215
  79.9 0.8 add_cores.1
  80.7 19.3 %all_to_all.10.sent = s16[4,1040,128]{2,1,0:T(8,128)(2,1)S(1)} all-to-all(s16[4,1040,128]{2,1,0:T(8,128)(2,1)S(1)} %add_cores.1), channel_id=1, replica_groups={{0,16,512,528},{32,48,544,560},{64,80,576,592},{96,112,608,624},{128,14..., dimensions={0} | all-to-all | bytes 2129920 | tf_op jit(solution)/shard_map/all_to_all | solution.py:228
  99.9 0.5 add_fours.1
  100.5 16.2 %all_to_all.11 = f16[16,64,128]{2,1,0:T(8,128)(2,1)S(1)} all-to-all(f16[16,64,128]{2,1,0:T(8,128)(2,1)S(1)} %convert_element_type.54), channel_id=1, replica_groups=mesh['island'=4,'fsdp'=16,'tensor'=16] {'fsdp'}, dimensions={0} | all-to-all | bytes 524288 | tf_op jit(solution)/shard_map/all_to_all | solution.py:237
  116.6 0.1 fusion
  116.7 13.9 %all_gather.8 = f32[4,128,128]{2,1,0:T(8,128)S(1)} all-gather(f32[1,128,128]{2,1,0:T(8,128)S(1)} %bitcast.53), channel_id=1, replica_groups=mesh['island'=4,'fsdp'=16,'tensor'=16] {'island'}, dimensions={0}, use_global_device_ids=true | all-gather | bytes 327680 | tf_op jit(solution)/shard_map/all_gather | solution.py:239
  130.6 0.0 copy-done.3
  130.6 0.9 fusion.4
  (10 shorter events, 0.1 us)
Async XLA Ops:
  54.3 12.1 %copy-start = (bf16[256,4608]{1,0:T(8,128)(2,1)S(1)}, bf16[256,4608]{1,0:T(8,128)(2,1)}, u32[]{:S(2)}) copy-start(bf16[256,4608]{1,0:T(8,128)(2,1)} %tok.3) | copy-start | bytes 7077892
  56.1 13.8 %collective-permute-start = (bf16[16,528,128]{2,1,0:T(8,128)(2,1)}, bf16[16,528,128]{2,1,0:T(8,128)(2,1)}, u32[]{:S(2)}, u32[]{:S(2)}) collective-permute-start(bf16[16,528,128]{2,1,0:T(8,128)(2,1)} %multiply_convert_fusion.sent), channel_id=1, source_target_pairs={{0,256},{256,0},{512,768},{768,512},{1,257},{257,1},{513,769},{769... | collective-permute-start | bytes 6488072 | tf_op jit(solution)/shard_map/ppermute | solution.py:185
  66.3 3.6 %copy-start.1 = (bf16[256,4608]{1,0:T(8,128)(2,1)S(1)}, bf16[256,4608]{1,0:T(8,128)(2,1)}, u32[]{:S(2)}) copy-start(bf16[256,4608]{1,0:T(8,128)(2,1)} %cot.3) | copy-start | bytes 7077892
  66.3 3.6 %copy-start.2 = (s32[64,1]{0,1:T(1,128)S(1)}, s32[64,1]{0,1:T(1,128)}, u32[]{:S(2)}) copy-start(s32[64,1]{0,1:T(1,128)} %param.15) | copy-start | bytes 772
  75.3 4.6 %collective-permute-start.1 = (s16[4128,128]{1,0:T(8,128)(2,1)S(1)}, s16[4128,128]{1,0:T(8,128)(2,1)S(1)}, u32[]{:S(2)}, u32[]{:S(2)}) collective-permute-start(s16[4128,128]{1,0:T(8,128)(2,1)S(1)} %get-tuple-element.5), channel_id=1, source_target_pairs={{0,256},{256,0},{512,768},{768,512},{1,257},{257,1},{513,769},{769... | collective-permute-start | bytes 3170312 | tf_op jit(solution)/shard_map/ppermute | solution.py:215
  99.9 30.7 %copy-start.3 = (f32[4,1,128,128]{3,2,1,0:T(8,128)S(1)}, f32[4,1,128,128]{3,2,1,0:T(8,128)}, u32[]{:S(2)}) copy-start(f32[4,1,128,128]{3,2,1,0:T(8,128)} %param.16) | copy-start | bytes 786436
  99.9 30.7 %copy-start.4 = (f32[4,1,128,128]{3,2,1,0:T(8,128)S(1)}, f32[4,1,128,128]{3,2,1,0:T(8,128)}, u32[]{:S(2)}) copy-start(f32[4,1,128,128]{3,2,1,0:T(8,128)} %param.17) | copy-start | bytes 786436
